TPU v7x, 32 devices: a whole 2x2x4 slice. The times are simulated.
32 devices in a mesh: dp: 2 (over y), node: 4 (over z), local: 4 (over x, core).
Axes of the slice: x: 2, y: 2, z: 4, core: 2. Of those that a mesh axis runs over, the one named last changes fastest.
Arguments:
- tokens: bfloat16 [512, 2048], P(('dp', 'node', 'local')), parts along dimension 0, may hold values from -6 to 6
- cotangent: bfloat16 [512, 2048], P(('dp', 'node', 'local')), parts along dimension 0, may hold values from -6 to 6
- expert_ids: int32 [512, 8], P(('dp', 'node', 'local')), parts along dimension 0, may hold values from 0 to 15, all different within a row; in each aligned block of 16 rows (0 to 15, 16 to 31, ...) at most 16 rows name the same one
- combine: float32 [512, 8], P(('dp', 'node', 'local')), parts along dimension 0, may hold values from 0.05 to 0.3
- w_gate_up: bfloat16 [16, 2048, 768], P(('node', 'local')), may hold values from -0.125 to 0.125
- w_down: bfloat16 [16, 384, 2048], P(('node', 'local')), may hold values from -0.3125 to 0.3125
Outputs:
- mixed: bfloat16 [512, 2048], P(('dp', 'node', 'local')), parts along dimension 0
- grad_tokens: bfloat16 [512, 2048], P(('dp', 'node', 'local')), parts along dimension 0
- grad_combine: float32 [512, 8], P(('dp', 'node', 'local')), parts along dimension 0
There are 2 independent parts, one for each index of `dp`. A program takes and returns all parts, laid end to end along the dimension named above; an argument that names none is the same for every part. Nothing has to cross between parts.
Inputs may be any that keep to these rules, and one draw needn't show every extreme that they name: `expert_ids`: each row names 8 different experts. Among the rows of one device no expert is named more than 16 times, a bound that some block reaches.
All inputs are finite; a program needn't handle non-finite values.
Results may differ from a plain program's by a relative error of at most 0.012.
Values may be sent and summed in bfloat16 or wider, within the bound.
A program may use at most 64 MiB of HBM per device.

v0:
```python
import jax
import jax.numpy as jnp
from jax import lax
from jax.sharding import PartitionSpec as P


def expert_forward(rows, w_gate_up, w_down):
    width = w_down.shape[0]
    projected = jnp.dot(rows, w_gate_up, preferred_element_type=jnp.float32)
    gate = projected[:, :width]
    upward = projected[:, width:]
    hidden = (gate * jax.nn.sigmoid(gate) * upward).astype(jnp.bfloat16)
    output = jnp.dot(hidden, w_down, preferred_element_type=jnp.float32).astype(jnp.bfloat16)
    return (output, gate, upward)


def expert_backward(grads, gate, upward, w_gate_up, w_down):
    grad_hidden = lax.dot_general(
        grads, w_down, (((1,), (1,)), ((), ())), preferred_element_type=jnp.float32
    )
    sigmoid = jax.nn.sigmoid(gate)
    grad_gate = grad_hidden * upward * sigmoid * (1.0 + gate * (1.0 - sigmoid))
    grad_up = grad_hidden * gate * sigmoid
    paired = jnp.concatenate([grad_gate, grad_up], axis=1).astype(jnp.bfloat16)
    back = lax.dot_general(
        paired, w_gate_up, (((1,), (1,)), ((), ())), preferred_element_type=jnp.float32
    )
    return back.astype(jnp.bfloat16)


def node_tables(ids_all, weights_all, node_here, node_count, local_count, capacity):
    rows_all, top_count = ids_all.shape
    tok_rows = rows_all // node_count
    experts = node_count * local_count
    per_source = ids_all.reshape(node_count, tok_rows * top_count)
    onehot = (per_source[:, :, None] == jnp.arange(experts, dtype=jnp.int32)[None, None, :]).astype(
        jnp.int32
    )
    before = jnp.cumsum(onehot, axis=1) - onehot
    ranks = jnp.sum(before * onehot, axis=2)
    source = jnp.arange(node_count, dtype=jnp.int32)[:, None]
    inside = per_source // local_count == node_here
    slots = per_source % local_count * (node_count * capacity) + source * capacity + ranks
    slots = jnp.where(inside, slots, -1).reshape(rows_all, top_count)
    matches = (
        slots[None, :, :]
        == jnp.arange(local_count * node_count * capacity, dtype=jnp.int32)[:, None, None]
    )
    placing = jnp.any(matches, axis=2).astype(jnp.bfloat16)
    slot_weight = jnp.sum(jnp.where(matches, weights_all[None, :, :], 0.0), axis=(1, 2))
    return (matches, placing, slot_weight)


def per_device(tokens, cotangent, expert_ids, combine, w_gate_up, w_down):
    node_count = lax.axis_size("node")
    local_count = lax.axis_size("local")
    experts = node_count * local_count
    tok_rows, top_count = expert_ids.shape
    width = tokens.shape[1]
    capacity = max(2, 2 * tok_rows * top_count // experts)
    gate_up_one = w_gate_up[0]
    down_one = w_down[0]
    route = jnp.concatenate([expert_ids.astype(jnp.float32), combine], axis=1)
    route_all = lax.all_gather(route, "node", axis=0, tiled=True)
    ids_all = route_all[:, :top_count].astype(jnp.int32)
    weights_all = route_all[:, top_count:]
    tokens_all, cot_all = (
        lax.all_gather(tokens, "node", axis=0, tiled=True),
        lax.all_gather(cotangent, "node", axis=0, tiled=True),
    )
    matches, placing, slot_weight = node_tables(
        ids_all, weights_all, lax.axis_index("node"), node_count, local_count, capacity
    )
    send_x = jnp.dot(placing, tokens_all, preferred_element_type=jnp.float32).astype(jnp.bfloat16)
    send_x = send_x.reshape(local_count, node_count * capacity, width)
    cot_rows = jnp.dot(placing, cot_all, preferred_element_type=jnp.float32)
    send_g = (cot_rows * slot_weight[:, None]).astype(jnp.bfloat16)
    send_g = send_g.reshape(local_count, node_count * capacity, width)
    arrived, arrived_grad = (
        lax.all_to_all(send_x, "local", split_axis=0, concat_axis=0, tiled=True),
        lax.all_to_all(send_g, "local", split_axis=0, concat_axis=0, tiled=True),
    )
    output, gate, upward = expert_forward(arrived.reshape(-1, width), gate_up_one, down_one)
    back = expert_backward(arrived_grad.reshape(-1, width), gate, upward, gate_up_one, down_one)
    output = output.reshape(local_count, node_count * capacity, width)
    back = back.reshape(local_count, node_count * capacity, width)
    came_back, back_home = (
        lax.all_to_all(output, "local", split_axis=0, concat_axis=0, tiled=True),
        lax.all_to_all(back, "local", split_axis=0, concat_axis=0, tiled=True),
    )
    flat_out = came_back.reshape(-1, width).astype(jnp.float32)
    flat_back = back_home.reshape(-1, width)
    gather_rows = placing.T
    mixed_part = jnp.dot(
        gather_rows.astype(jnp.float32),
        flat_out * slot_weight[:, None],
        precision=lax.Precision.HIGHEST,
    )
    back_part = jnp.dot(gather_rows, flat_back, preferred_element_type=jnp.float32)
    slot_dot = jnp.sum(cot_rows * flat_out, axis=1)
    combine_part = jnp.sum(jnp.where(matches, slot_dot[:, None, None], 0.0), axis=0)
    mixed, grad_tokens, grad_combine = (
        lax.psum_scatter(mixed_part, "node", scatter_dimension=0, tiled=True),
        lax.psum_scatter(back_part, "node", scatter_dimension=0, tiled=True),
        lax.psum_scatter(combine_part, "node", scatter_dimension=0, tiled=True),
    )
    return (mixed.astype(jnp.bfloat16), grad_tokens.astype(jnp.bfloat16), grad_combine)


def solution(mesh):
    placed = (
        P(("dp", "node", "local"), None),
        P(("dp", "node", "local"), None),
        P(("dp", "node", "local"), None),
        P(("dp", "node", "local"), None),
        P(("node", "local"), None, None),
        P(("node", "local"), None, None),
    )
    return jax.shard_map(
        per_device,
        mesh=mesh,
        in_specs=placed,
        out_specs=(
            P(("dp", "node", "local"), None),
            P(("dp", "node", "local"), None),
            P(("dp", "node", "local"), None),
        ),
        check_vma=False,
    )
```

profile of v0, /device:TPU:0, one launch (start us, length us, event | category | flops | bytes accessed | tf_op | source)
XLA Modules:
  0.0 168.9 jit_solution(520398317080395630)
XLA Ops:
  7.2 0.0 copy-start
  7.2 0.8 convert_element_type.39
  8.0 0.8 pad_maximum_fusion
  8.8 0.1 copy.23
  8.9 14.8 %all_gather.9 = f32[64,16]{1,0:T(8,128)S(1)} all-gather(f32[16,16]{1,0:T(8,128)S(1)} %copy.23), channel_id=1, replica_groups=mesh['dp'=2,'node'=4,'local'=4] {'node'}, dimensions={0}, use_global_device_ids=true | all-gather | bytes 5120 | tf_op jit(solution)/shard_map/all_gather | solution.py:64
  23.7 0.1 fusion.28
  23.8 0.1 eq.40
  23.9 0.8 fusion.17
  24.7 1.2 reduce_window_sum.11
  25.9 0.2 select_reduce_fusion.2
  26.2 0.1 reduce_sum.39
  26.3 0.1 add.44
  26.3 0.1 add.45
  26.4 0.1 fusion.23
  26.5 0.2 fusion.13
  26.7 14.5 %all_gather.10 = bf16[64,2048]{1,0:T(8,128)(2,1)S(1)} all-gather(bf16[16,2048]{1,0:T(8,128)(2,1)} %param.6), channel_id=1, replica_groups=mesh['dp'=2,'node'=4,'local'=4] {'node'}, dimensions={0}, use_global_device_ids=true | all-gather | bytes 327680 | tf_op jit(solution)/shard_map/all_gather | solution.py:68
  41.3 0.5 convolution_convert_fusion.1
  41.8 17.0 %all_to_all.20 = bf16[4,64,2048]{2,1,0:T(8,128)(2,1)S(1)} all-to-all(bf16[4,64,2048]{2,1,0:T(8,128)(2,1)S(1)} %bitcast.35), channel_id=1, replica_groups=mesh['dp'=2,'node'=4,'local'=4] {'local'}, dimensions={0} | all-to-all | bytes 2097152 | tf_op jit(solution)/shard_map/all_to_all | solution.py:80
  58.8 0.0 copy-done
  58.8 0.0 copy-start.1
  58.8 1.0 fusion.2
  59.8 0.4 copy-done.1
  60.2 0.0 copy-start.2
  60.2 1.8 %convolution_convert_fusion = bf16[256,2048]{1,0:T(8,128)(2,1)} fusion(bf16[1,384,2048]{2,1,0:T(8,128)(2,1)S(1)} %copy-done.1, f32[256,768]{1,0:T(8,128)S(1)} %fusion.2), kind=kOutput, calls=%fused_computation.6 | convolution fusion | flops 403767296 | bytes 3407872 | tf_op jit(solution)/shard_map/dot_general | solution.py:13
  62.0 0.0 copy-done.2
  62.0 4.2 %all-to-all-start.1 = ((bf16[4,64,2048]{2,1,0:T(8,128)(2,1)}), bf16[4,64,2048]{2,1,0:T(8,128)(2,1)}, u32[]{:S(2)}, u32[]{:S(2)}) async-start(bf16[4,64,2048]{2,1,0:T(8,128)(2,1)} %bitcast.37), calls=%async_computation.1 | async-start | bytes 2097152 | tf_op jit(solution)/shard_map/all_to_all | solution.py:88
  66.2 14.3 %all_gather.11 = bf16[64,2048]{1,0:T(8,128)(2,1)S(1)} all-gather(bf16[16,2048]{1,0:T(8,128)(2,1)} %param.7), channel_id=1, replica_groups=mesh['dp'=2,'node'=4,'local'=4] {'node'}, dimensions={0}, use_global_device_ids=true | all-gather | bytes 327680 | tf_op jit(solution)/shard_map/all_gather | solution.py:69
  80.5 0.2 all-to-all-done.1
  80.7 1.8 %fusion.8 = (f32[256]{0:T(256)S(1)}, f32[256,2048]{1,0:T(8,128)S(1)}) fusion(bf16[4,64,2048]{2,1,0:T(8,128)(2,1)} %all-to-all-done.1, pred[256,64]{0,1:T(8,128)(4,1)S(1)} %fusion.13, bf16[64,2048]{1,0:T(8,128)(2,1)S(1)} %all_gather.11), kind=kOutput, calls=%fused_computation.10 | convolution fusion | flops 68681472 | bytes 3425280 | tf_op jit(solution)/shard_map/dot_general | solution.py:76
  82.5 0.9 select_reduce_fusion
  83.4 1.2 multiply_convert_fusion
  84.6 4.3 %all-to-all-start.2 = ((bf16[4,64,2048]{2,1,0:T(8,128)(2,1)}), bf16[4,64,2048]{2,1,0:T(8,128)(2,1)}, u32[]{:S(2)}, u32[]{:S(2)}) async-start(bf16[4,64,2048]{2,1,0:T(8,128)(2,1)} %bitcast.34), calls=%async_computation.3 | async-start | bytes 2097152 | tf_op jit(solution)/shard_map/all_to_all | solution.py:81
  88.9 0.0 reduce-scatter.10.cloned.1.call-start
  88.9 0.7 reduce-scatter.10.cloned.1.call-update
  89.6 13.8 %all-to-all-done.2 = bf16[4,64,2048]{2,1,0:T(8,128)(2,1)} async-done(((bf16[4,64,2048]{2,1,0:T(8,128)(2,1)}), bf16[4,64,2048]{2,1,0:T(8,128)(2,1)}, u32[]{:S(2)}, u32[]{:S(2)}) %all-to-all-start.2) | async-done | bytes 1048608 | tf_op jit(solution)/shard_map/all_to_all | solution.py:81
  103.4 2.7 %multiply_convert_fusion.2 = (bf16[256,384]{1,0:T(8,128)(2,1)S(1)}, bf16[256,384]{1,0:T(8,128)(2,1)S(1)}) fusion(f32[256,768]{1,0:T(8,128)} %copy-done.2, bf16[256,2048]{1,0:T(8,128)(2,1)} %bitcast.7, bf16[1,384,2048]{2,1,0:T(8,128)(2,1)} %param.11), kind=kOutput, calls=%fused_computation.24 | convolution fusion | flops 403931136 | bytes 3801088 | tf_op jit(solution)/shard_map/dot_general | solution.py:18
  106.1 2.0 %fusion.4 = bf16[256,2048]{1,0:T(8,128)(2,1)} fusion(bf16[1,2048,768]{2,1,0:T(8,128)(2,1)S(1)} %copy-done, bf16[256,384]{1,0:T(8,128)(2,1)S(1)} %get-tuple-element.6, bf16[256,384]{1,0:T(8,128)(2,1)S(1)} %get-tuple-element.5), kind=kOutput, calls=%fused_computation.7 | convolution fusion | flops 806617088 | bytes 4587520 | tf_op jit(solution)/shard_map/dot_general | solution.py:25
  108.1 4.3 %all-to-all-start.3 = ((bf16[4,64,2048]{2,1,0:T(8,128)(2,1)}), bf16[4,64,2048]{2,1,0:T(8,128)(2,1)}, u32[]{:S(2)}, u32[]{:S(2)}) async-start(bf16[4,64,2048]{2,1,0:T(8,128)(2,1)} %bitcast.36), calls=%async_computation.4 | async-start | bytes 2097152 | tf_op jit(solution)/shard_map/all_to_all | solution.py:89
  112.4 0.0 reduce-scatter.6.cloned.1.call-start
  112.4 3.1 %fusion.7 = f32[64,2048]{1,0:T(8,128)} fusion(pred[256,64]{0,1:T(8,128)(4,1)S(1)} %fusion.13, bf16[256,2048]{1,0:T(8,128)(2,1)} %bitcast.10, f32[256]{0:T(256)S(1)} %get-tuple-element.4), kind=kOutput, calls=%fused_computation.9 | convolution fusion | flops 403701760 | bytes 1590272 | tf_op jit(solution)/shard_map/dot_general | solution.py:94
  115.5 0.0 reduce-scatter.6.cloned.1.call-update
  115.6 0.0 reduce-scatter.8.cloned.1.call-start
  115.6 11.3 %all-to-all-done.3 = bf16[4,64,2048]{2,1,0:T(8,128)(2,1)} async-done(((bf16[4,64,2048]{2,1,0:T(8,128)(2,1)}), bf16[4,64,2048]{2,1,0:T(8,128)(2,1)}, u32[]{:S(2)}, u32[]{:S(2)}) %all-to-all-start.3) | async-done | bytes 1048608 | tf_op jit(solution)/shard_map/all_to_all | solution.py:89
  126.9 2.3 %fusion.29 = f32[64,2048]{1,0:T(8,128)} fusion(pred[256,64]{0,1:T(8,128)(4,1)S(1)} %fusion.13, bf16[256,2048]{1,0:T(8,128)(2,1)} %bitcast.9), kind=kOutput, calls=%fused_computation.50 | convolution fusion | flops 67108864 | bytes 1589248 | tf_op jit(solution)/shard_map/dot_general | solution.py:99
  129.2 0.0 reduce-scatter.8.cloned.1.call-update
  129.2 0.0 reduce-scatter.10.cloned.1.call-done
  129.2 1.4 copy.26
  130.6 7.8 %reduce-scatter.6.cloned.1.call-done = f32[16,2048]{1,0:T(8,128)} async-done(((f32[64,2048]{1,0:T(8,128)}), f32[16,2048]{1,0:T(8,128)}) %reduce-scatter.6.cloned.1.call-update) | async-done | bytes 131088 | tf_op jit(solution)/shard_map/reduce_scatter | solution.py:103
  138.4 1.5 convert_element_type.47
  139.9 20.9 %reduce-scatter.8.cloned.1.call-done = f32[16,2048]{1,0:T(8,128)} async-done(((f32[64,2048]{1,0:T(8,128)}), f32[16,2048]{1,0:T(8,128)}) %reduce-scatter.8.cloned.1.call-update) | async-done | bytes 131088 | tf_op jit(solution)/shard_map/reduce_scatter | solution.py:104
  160.8 1.5 convert_element_type.50
  (1 shorter events, 0.0 us)
Async XLA Ops:
  7.2 51.6 %copy-start = (bf16[1,2048,768]{2,1,0:T(8,128)(2,1)S(1)}, bf16[1,2048,768]{2,1,0:T(8,128)(2,1)}, u32[]{:S(2)}) copy-start(bf16[1,2048,768]{2,1,0:T(8,128)(2,1)} %param.10) | copy-start | bytes 9437188
  58.8 1.4 copy-start.1
  60.2 1.8 %copy-start.2 = (f32[256,768]{1,0:T(8,128)}, f32[256,768]{1,0:T(8,128)S(1)}, u32[]{:S(2)}) copy-start(f32[256,768]{1,0:T(8,128)S(1)} %fusion.2) | copy-start | bytes 2359300
  62.0 18.8 %all-to-all-start.1 = ((bf16[4,64,2048]{2,1,0:T(8,128)(2,1)}), bf16[4,64,2048]{2,1,0:T(8,128)(2,1)}, u32[]{:S(2)}, u32[]{:S(2)}) async-start(bf16[4,64,2048]{2,1,0:T(8,128)(2,1)} %bitcast.37), calls=%async_computation.1 | async-start | bytes 2097152 | tf_op jit(solution)/shard_map/all_to_all | solution.py:88
  84.6 18.8 %all-to-all-start.2 = ((bf16[4,64,2048]{2,1,0:T(8,128)(2,1)}), bf16[4,64,2048]{2,1,0:T(8,128)(2,1)}, u32[]{:S(2)}, u32[]{:S(2)}) async-start(bf16[4,64,2048]{2,1,0:T(8,128)(2,1)} %bitcast.34), calls=%async_computation.3 | async-start | bytes 2097152 | tf_op jit(solution)/shard_map/all_to_all | solution.py:81
  88.9 40.4 %reduce-scatter.10.cloned.1.call-start = ((), (), s32[]{:S(2)}) async-start(), calls=%async_computation.9 | async-start | bytes 40960
  108.1 18.8 %all-to-all-start.3 = ((bf16[4,64,2048]{2,1,0:T(8,128)(2,1)}), bf16[4,64,2048]{2,1,0:T(8,128)(2,1)}, u32[]{:S(2)}, u32[]{:S(2)}) async-start(bf16[4,64,2048]{2,1,0:T(8,128)(2,1)} %bitcast.36), calls=%async_computation.4 | async-start | bytes 2097152 | tf_op jit(solution)/shard_map/all_to_all | solution.py:89
  112.4 26.0 %reduce-scatter.6.cloned.1.call-start = ((), (), s32[]{:S(2)}) async-start(), calls=%async_computation.7 | async-start | bytes 655360 | tf_op jit(solution)/shard_map/reduce_scatter | solution.py:103
  115.6 45.3 %reduce-scatter.8.cloned.1.call-start = ((), (), s32[]{:S(2)}) async-start(), calls=%async_computation.8 | async-start | bytes 655360 | tf_op jit(solution)/shard_map/reduce_scatter | solution.py:104
Sparse Core Ops, SparseCore 0:
  92.5 20.1 reduce-scatter.9
  115.7 22.6 reduce-scatter.5
  140.8 20.0 reduce-scatter.7
where the time goes:
time: 170 us; the launch traced here: 169 us
  blocking collectives  60.6 us (36%)
  waiting for transfers between devices  54.7 us (32%)
  matrix products  15.1 us (9%)
  between operations  13.8 us (8%)
  starting transfers between devices  12.9 us (8%)
  other arithmetic  9.49 us (6%)
  local copies, waits for them, and re-layouts  2.21 us (1%)
    reduce_scatter x1, waiting for transfers between devices, per_device(): lax.psum_scatter(back_part, 'node', scatter_dimension=0, tiled=True)  20.9 us
    all_to_all x1, blocking collectives, per_device(): lax.all_to_all(send_x, 'local', split_axis=0, concat_axis=0, tiled=True)  17 us
    all_gather x1, blocking collectives, per_device(): route_all = lax.all_gather(route, 'node', axis=0, tiled=True)  14.8 us
    all_gather x1, blocking collectives, per_device(): lax.all_gather(tokens, 'node', axis=0, tiled=True)  14.5 us
    all_gather x1, blocking collectives, per_device(): lax.all_gather(cotangent, 'node', axis=0, tiled=True)  14.3 us
    all_to_all x1, waiting for transfers between devices, per_device(): lax.all_to_all(send_g, 'local', split_axis=0, concat_axis=0, tiled=True)  13.8 us
    all_to_all x1, waiting for transfers between devices, per_device(): lax.all_to_all(back, 'local', split_axis=0, concat_axis=0, tiled=True)  11.3 us
    reduce_scatter x1, waiting for transfers between devices, per_device(): lax.psum_scatter(mixed_part, 'node', scatter_dimension=0, tiled=True)  7.78 us
  transfers between devices with their start and end apart: 6, of which 5 were waited for; matrix products, arithmetic and copies ran while one was open for 8% of the time, Pallas kernels for 0%

commit v1 on v0

--- a/solution.py
+++ b/solution.py
@@ -1,7 +1,16 @@
+import functools
+
 import jax
 import jax.numpy as jnp
 from jax import lax
+from jax.experimental import pallas as pl
+from jax.experimental.pallas import tpu as pltpu
 from jax.sharding import PartitionSpec as P
+
+MESH = pl.DeviceIdType.MESH
+LANES = 128
+F32 = jnp.float32
+BF16 = jnp.bfloat16
 
 
 def expert_forward(rows, w_gate_up, w_down):
@@ -107,6 +116,349 @@
     return (mixed.astype(jnp.bfloat16), grad_tokens.astype(jnp.bfloat16), grad_combine)
 
 
+def dense_kernel(
+    n,
+    tok_ref,
+    cot_ref,
+    ids_ref,
+    comb_ref,
+    gate_up_hbm,
+    down_hbm,
+    mixed_ref,
+    grad_ref,
+    gcomb_ref,
+    wgu,
+    wd,
+    xs,
+    cs,
+    pm,
+    pb,
+    gate_s,
+    up_s,
+    hid_s,
+    cr_m,
+    cr_b,
+    xs_m,
+    xs_b,
+    xr_m,
+    xr_b,
+    zs_m,
+    zs_b,
+    zr_m,
+    zr_b,
+    w_sem,
+    ag_send,
+    ag_recv,
+    core_send,
+    core_recv,
+    x_send,
+    x_recv,
+    z_send,
+    z_recv,
+):
+    tok, width = tok_ref.shape
+    top = ids_ref.shape[1]
+    ff = wd.shape[0]
+    z = lax.axis_index("node")
+    local = lax.axis_index("local")
+    x, c = local // 2, local % 2
+    experts = n * 4
+    me = z * 4 + local
+    half = 2 * n * tok
+    quarter = n * tok
+
+    partner = {"local": (1 - x) * 2 + c}
+    sibling = {"local": x * 2 + 1 - c}
+
+    def zdev(d):
+        return {"node": lax.rem(z + d, n)}
+
+    def column(xx, cc):
+        return pl.multiple_of((xx * 2 + cc) * quarter, quarter)
+
+    def rows(xx, cc, zz):
+        return pl.ds(pl.multiple_of(((xx * 2 + cc) * n + zz) * tok, tok), tok)
+
+    load_gu = pltpu.make_async_copy(gate_up_hbm.at[0], wgu, w_sem.at[0])
+    load_d = pltpu.make_async_copy(down_hbm.at[0], wd, w_sem.at[1])
+    load_gu.start()
+    load_d.start()
+
+    barrier = pltpu.get_barrier_semaphore()
+    for d in range(1, n):
+        pl.semaphore_signal(barrier, inc=1, device_id=zdev(d), device_id_type=MESH)
+    pl.semaphore_signal(barrier, inc=1, device_id=partner, device_id_type=MESH)
+    pl.semaphore_signal(barrier, inc=1, device_id=sibling, device_id_type=MESH)
+
+    mine = rows(x, c, z)
+    lane = lax.broadcasted_iota(jnp.int32, (tok, LANES), 1)
+    lane_expert = jnp.where(lane < experts, lane, lane - experts)
+    ids = ids_ref[...]
+    comb = comb_ref[...]
+    weight = jnp.zeros((tok, LANES), F32)
+    for k in range(top):
+        weight = weight + jnp.where(ids[:, k : k + 1] == lane_expert, comb[:, k : k + 1], 0.0)
+    coarse = weight.astype(BF16).astype(F32)
+    xs[mine, :width] = tok_ref[...]
+    xs[mine, width:] = jnp.where(lane < experts, coarse, weight - coarse).astype(BF16)
+    cs[mine, :] = cot_ref[...]
+    pl.semaphore_wait(barrier, n + 1)
+
+    sends = []
+
+    def remote(src, dst, send_sem, recv_sem, device):
+        return pltpu.make_async_remote_copy(
+            src_ref=src,
+            dst_ref=dst,
+            send_sem=send_sem,
+            recv_sem=recv_sem,
+            device_id=device,
+            device_id_type=MESH,
+        )
+
+    def go(*args):
+        copy = remote(*args)
+        copy.start()
+        sends.append(copy)
+
+    bufs = (xs, cs)
+
+    def gather_go(t, role, d, where, device):
+        go(bufs[t].at[where], bufs[t].at[where], ag_send.at[t, role, d], ag_recv.at[t, role, d], device)
+
+    def gather_wait(t, role, d, where):
+        remote(
+            bufs[t].at[where], bufs[t].at[where], ag_send.at[t, role, d], ag_recv.at[t, role, d], sibling
+        ).wait_recv()
+
+    def back_by(d):
+        return lax.rem(z + n - d, n)
+
+    for t in range(2):
+        gather_go(t, 1, 0, mine, partner)
+        for d in range(1, n):
+            gather_go(t, 0, d, mine, zdev(d))
+        gather_go(t, 2, 0, mine, sibling)
+
+    def pass_z(t):
+        for d in range(1, n):
+            where = rows(x, c, back_by(d))
+            gather_wait(t, 0, d, where)
+            gather_go(t, 1, d, where, partner)
+            gather_go(t, 2, d, where, sibling)
+
+    def pass_x(t):
+        for d in range(n):
+            where = rows(1 - x, c, back_by(d))
+            gather_wait(t, 1, d, where)
+            gather_go(t, 3, d, where, sibling)
+
+    def await_sibling(t, other):
+        for d in range(n):
+            where = rows(1 - x if other else x, 1 - c, back_by(d))
+            gather_wait(t, 3 if other else 2, d, where)
+
+    tile = 512 if width % 512 == 0 else width
+    wide_lane = lax.broadcasted_iota(jnp.int32, (half, LANES), 1)
+
+    def chunk(other):
+        return pl.ds(pl.multiple_of((1 - x if other else x) * half, half), half)
+
+    def my_weight(r):
+        block = xs[r, width:].astype(F32)
+        chosen = (wide_lane == me) | (wide_lane == me + experts)
+        return jnp.sum(jnp.where(chosen, block, 0.0), axis=1, keepdims=True)
+
+    def forward(other):
+        r = chunk(other)
+        projected = jnp.dot(xs[r, :width], wgu[...], preferred_element_type=F32)
+        gate = projected[:, :ff]
+        upward = projected[:, ff:]
+        hidden = (gate * jax.nn.sigmoid(gate) * upward).astype(BF16)
+        gate_s[r, :] = gate
+        up_s[r, :] = upward
+        hid_s[r, :] = hidden
+        weight = my_weight(r)
+        for j in range(width // tile):
+            cols = slice(j * tile, (j + 1) * tile)
+            out = jnp.dot(hidden, wd[:, cols], preferred_element_type=F32)
+            pm[r, cols] = (out * weight).astype(BF16)
+
+    across = (((1,), (1,)), ((), ()))
+
+    def backward(other):
+        r = chunk(other)
+        plain = lax.dot_general(cs[r, :], wd[...], across, preferred_element_type=F32)
+        gate = gate_s[r, :]
+        upward = up_s[r, :]
+        grads = plain * my_weight(r)
+        sig = jax.nn.sigmoid(gate)
+        grad_gate = grads * upward * sig * (1.0 + gate * (1.0 - sig))
+        grad_up = grads * gate * sig
+        dots = jnp.sum(plain * hid_s[r, :].astype(F32), axis=1, keepdims=True)
+        coarse = dots.astype(BF16).astype(F32)
+        pb[r, width:] = jnp.where(
+            wide_lane == me, coarse, jnp.where(wide_lane == me + experts, dots - coarse, 0.0)
+        ).astype(BF16)
+        paired = jnp.concatenate([grad_gate, grad_up], axis=1).astype(BF16)
+        for j in range(width // tile):
+            cols = slice(j * tile, (j + 1) * tile)
+            back = lax.dot_general(paired, wgu[cols, :], across, preferred_element_type=F32)
+            pb[r, cols] = back.astype(BF16)
+
+    parts, from_core = (pm, pb), (cr_m, cr_b)
+    to_x, from_x = (xs_m, xs_b), (xr_m, xr_b)
+    to_z, from_z = (zs_m, zs_b), (zr_m, zr_b)
+
+    def core_copy(t, other):
+        src = parts[t].at[pl.ds(column(1 - x if other else x, 1 - c), quarter)]
+        q = 1 if other else 0
+        return (src, from_core[t].at[q], core_send.at[t, q], core_recv.at[t, q], sibling)
+
+    def core_go(t, other):
+        go(*core_copy(t, other))
+
+    def core_wait(t, other):
+        remote(*core_copy(t, other)).wait_recv()
+
+    def core_rows(d):
+        return pl.ds(pl.multiple_of(lax.rem(z + d, n) * tok, tok), tok)
+
+    def x_copy(t, d):
+        return (to_x[t].at[d], from_x[t].at[d], x_send.at[t, d], x_recv.at[t, d], partner)
+
+    def z_copy(t, d):
+        return (to_z[t].at[d], from_z[t].at[d], z_send.at[t, d], z_recv.at[t, d], zdev(d))
+
+    order = [d for d in range(1, n)] + [0]
+
+    def send_x(t):
+        core_wait(t, True)
+        for d in order:
+            own = parts[t][rows(1 - x, c, lax.rem(z + d, n)), :].astype(F32)
+            to_x[t][d] = (own + from_core[t][1, core_rows(d), :].astype(F32)).astype(BF16)
+            go(*x_copy(t, d))
+
+    def joined(t, d):
+        own = parts[t][rows(x, c, lax.rem(z + d, n)), :].astype(F32)
+        return own + from_core[t][0, core_rows(d), :].astype(F32) + from_x[t][d].astype(F32)
+
+    def send_z(t):
+        core_wait(t, False)
+        for d in order:
+            remote(*x_copy(t, d)).wait_recv()
+            if d > 0:
+                to_z[t][d] = joined(t, d).astype(BF16)
+                go(*z_copy(t, d))
+
+    def finish(t):
+        total = joined(t, 0)
+        for d in range(1, n):
+            remote(*z_copy(t, d)).wait_recv()
+            total = total + from_z[t][d].astype(F32)
+        return total
+
+    pass_z(0)
+    pass_z(1)
+    load_gu.wait()
+    load_d.wait()
+    pass_x(0)
+    await_sibling(0, False)
+    forward(False)
+    core_go(0, False)
+    await_sibling(0, True)
+    forward(True)
+    core_go(0, True)
+    await_sibling(1, False)
+    backward(False)
+    core_go(1, False)
+    send_x(0)
+    pass_x(1)
+    await_sibling(1, True)
+    backward(True)
+    core_go(1, True)
+    send_x(1)
+    send_z(0)
+    mixed_ref[...] = finish(0).astype(mixed_ref.dtype)
+    send_z(1)
+    total = finish(1)
+    grad_ref[...] = total[:, :width].astype(grad_ref.dtype)
+    dots = total[:, width:]
+    place = lax.broadcasted_iota(jnp.int32, (tok, top), 1)
+    picked = jnp.zeros((tok, top), F32)
+    for k in range(top):
+        value = jnp.sum(jnp.where(ids[:, k : k + 1] == lane_expert, dots, 0.0), axis=1, keepdims=True)
+        picked = picked + jnp.where(place == k, value, 0.0)
+    gcomb_ref[...] = picked
+    for copy in sends:
+        copy.wait_send()
+
+
+def dense_plan(tokens, cotangent, expert_ids, combine, w_gate_up, w_down):
+    n = lax.axis_size("node")
+    tok, width = tokens.shape
+    top = expert_ids.shape[1]
+    ff = w_down.shape[1]
+    total = 4 * n * tok
+    wide = width + LANES
+    vmem = pl.BlockSpec(memory_space=pltpu.VMEM)
+    hbm = pl.BlockSpec(memory_space=pl.ANY)
+    dma = pltpu.SemaphoreType.DMA
+    return pl.pallas_call(
+        functools.partial(dense_kernel, n),
+        out_shape=(
+            jax.ShapeDtypeStruct((tok, width), BF16),
+            jax.ShapeDtypeStruct((tok, width), BF16),
+            jax.ShapeDtypeStruct((tok, top), F32),
+        ),
+        in_specs=[vmem, vmem, vmem, vmem, hbm, hbm],
+        out_specs=(vmem, vmem, vmem),
+        scratch_shapes=[
+            pltpu.VMEM((width, 2 * ff), BF16),
+            pltpu.VMEM((ff, width), BF16),
+            pltpu.VMEM((total, wide), BF16),
+            pltpu.VMEM((total, width), BF16),
+            pltpu.VMEM((total, width), BF16),
+            pltpu.VMEM((total, wide), BF16),
+            pltpu.VMEM((total, ff), F32),
+            pltpu.VMEM((total, ff), F32),
+            pltpu.VMEM((total, ff), BF16),
+            pltpu.VMEM((2, n * tok, width), BF16),
+            pltpu.VMEM((2, n * tok, wide), BF16),
+            pltpu.VMEM((n, tok, width), BF16),
+            pltpu.VMEM((n, tok, wide), BF16),
+            pltpu.VMEM((n, tok, width), BF16),
+            pltpu.VMEM((n, tok, wide), BF16),
+            pltpu.VMEM((n, tok, width), BF16),
+            pltpu.VMEM((n, tok, wide), BF16),
+            pltpu.VMEM((n, tok, width), BF16),
+            pltpu.VMEM((n, tok, wide), BF16),
+            dma((2,)),
+            dma((2, 4, n)),
+            dma((2, 4, n)),
+            dma((2, 2)),
+            dma((2, 2)),
+            dma((2, n)),
+            dma((2, n)),
+            dma((2, n)),
+            dma((2, n)),
+        ],
+        compiler_params=pltpu.CompilerParams(
+            collective_id=0, has_side_effects=True, vmem_limit_bytes=40 * 1024 * 1024
+        ),
+    )(tokens, cotangent, expert_ids, combine, w_gate_up, w_down)
+
+
+def choose_plan(tokens, cotangent, expert_ids, combine, w_gate_up, w_down):
+    local_count = lax.axis_size("local")
+    experts = lax.axis_size("node") * local_count
+    tok_rows, top_count = expert_ids.shape
+    capacity = max(2, 2 * tok_rows * top_count // experts)
+    dense = capacity >= tok_rows and local_count == 4 and 2 * experts <= LANES and tok_rows % 16 == 0
+    plan = dense_plan if dense else per_device
+    return plan(tokens, cotangent, expert_ids, combine, w_gate_up, w_down)
+
+
 def solution(mesh):
     placed = (
         P(("dp", "node", "local"), None),
@@ -117,7 +469,7 @@
         P(("node", "local"), None, None),
     )
     return jax.shard_map(
-        per_device,
+        choose_plan,
         mesh=mesh,
         in_specs=placed,
         out_specs=(

time: 170 us -> 54.3 us (0.32)
  blocking collectives: 60.6 us -> 0 us
  waiting for transfers between devices: 54.7 us -> 0 us
  Pallas kernels: 0 us -> 44.9 us
  matrix products: 15.1 us -> 0 us
  between operations: 13.8 us -> 0.64 us
  starting transfers between devices: 12.9 us -> 0 us
  other arithmetic: 9.49 us -> 0 us
  local copies, waits for them, and re-layouts: 2.21 us -> 8.41 us
    pallas_call x0 -> x1, Pallas kernels: none -> 44.9 us  [dense_plan(): pl.pallas_call(functools.partial(dense_kernel, n), out_shape=(jax.ShapeDt...]
    all_gather x3 -> x0, blocking collectives: 43.6 us -> none  [the longest x1 14.8 us: per_device(): route_all = lax.all_gather(route, 'node', axis=0, tiled=True)]
    reduce_scatter x2 -> x0, waiting for transfers between devices: 28.7 us -> none  [the longest x1 20.9 us: per_device(): lax.psum_scatter(back_part, 'node', scatter_dimension=0, tiled=True)]
    all_to_all x3 -> x0, waiting for transfers between devices: 25.3 us -> none  [the longest x1 13.8 us: per_device(): lax.all_to_all(send_g, 'local', split_axis=0, concat_axis=0, tiled=True)]
    all_to_all x1 -> x0, blocking collectives: 17 us -> none  [per_device(): lax.all_to_all(send_x, 'local', split_axis=0, concat_axis=0, tiled=True)]
    dot_general x8 -> x0, matrix products: 15.1 us -> none  [the longest x1 3.13 us: per_device(): jnp.dot(gather_rows.astype(jnp.float32), flat_out * slot_weight[:, None],...]
    all_to_all x3 -> x0, starting transfers between devices: 12.8 us -> none  [the longest x1 4.26 us: per_device(): lax.all_to_all(send_g, 'local', split_axis=0, concat_axis=0, tiled=True)]
    unnamed x7 -> x12, local copies, waits for them, and re-layouts: 1.8 us -> 7.75 us
  transfers between devices with their start and end apart: 6 -> 0, of which waited for: 5 -> 0; matrix products, arithmetic and copies ran while one was open for 8% -> 0% of each run, Pallas kernels for 0% -> 0%
where the time goes in v1:
time: 54.3 us; the launch traced here: 53.9 us
  Pallas kernels  44.9 us (83%)
  local copies, waits for them, and re-layouts  8.41 us (15%)
  between operations  0.64 us (1%)
    pallas_call x1, Pallas kernels, dense_plan(): pl.pallas_call(functools.partial(dense_kernel, n), out_shape=(jax.ShapeDt...  44.9 us
    unnamed x12, local copies, waits for them, and re-layouts  7.75 us

profile of v1, /device:TPU:0, one launch (start us, length us, event | category | flops | bytes accessed | tf_op | source)
XLA Modules:
  0.0 53.9 jit_solution(11996922284838710314)
XLA Ops:
  0.6 0.8 %copy.9.ids_ref = s32[16,8]{1,0:T(8,128)S(1)} copy(s32[16,8]{0,1:T(8,128)} %param.8) | data formatting | bytes 1024 | tf_op args[2]
  1.4 0.8 %copy.10.comb_ref = f32[16,8]{1,0:T(8,128)S(1)} copy(f32[16,8]{0,1:T(8,128)} %param.9) | data formatting | bytes 1024 | tf_op args[3]
  2.1 0.0 copy-start
  2.1 1.9 %copy-done = bf16[1,2048,768]{2,1,0:T(8,128)(2,1)S(1)} copy-done((bf16[1,2048,768]{2,1,0:T(8,128)(2,1)S(1)}, bf16[1,2048,768]{2,1,0:T(8,128)(2,1)}, u32[]{:S(2)}) %copy-start) | copy-done | bytes 3145752
  4.0 0.0 copy-start.1
  4.0 1.4 %copy-done.1 = bf16[1,384,2048]{2,1,0:T(8,128)(2,1)S(1)} copy-done((bf16[1,384,2048]{2,1,0:T(8,128)(2,1)S(1)}, bf16[1,384,2048]{2,1,0:T(8,128)(2,1)}, u32[]{:S(2)}) %copy-start.1) | copy-done | bytes 1572888
  5.4 0.0 copy-start.2
  5.4 0.8 %copy-done.2 = bf16[16,2048]{1,0:T(8,128)(2,1)S(1)} copy-done((bf16[16,2048]{1,0:T(8,128)(2,1)S(1)}, bf16[16,2048]{1,0:T(8,128)(2,1)}, u32[]{:S(2)}) %copy-start.2) | copy-done | bytes 65560
  6.3 0.0 copy-start.3
  6.3 0.8 %copy-done.3 = bf16[16,2048]{1,0:T(8,128)(2,1)S(1)} copy-done((bf16[16,2048]{1,0:T(8,128)(2,1)S(1)}, bf16[16,2048]{1,0:T(8,128)(2,1)}, u32[]{:S(2)}) %copy-start.3) | copy-done | bytes 65560
  7.1 44.9 %shard_map.85 = (bf16[16,2048]{1,0:T(8,128)(2,1)S(1)}, bf16[16,2048]{1,0:T(8,128)(2,1)S(1)}, f32[16,8]{1,0:T(8,128)S(1)}) custom-call(bf16[16,2048]{1,0:T(8,128)(2,1)S(1)} %copy-done.2, bf16[16,2048]{1,0:T(8,128)(2,1)S(1)} %copy-done.3, s32[16,8]{1,0:T(8,128)S(1)} %copy.9.ids_ref, f32[16,8]{1,0:T(8,128)S(1)} %copy.10.comb_ref, ...), custom_call_target="tpu_custom_call" | custom-call | tf_op jit(solution)/shard_map/pallas_call | solution.py:407
  52.0 0.7 %copy.11 = f32[16,8]{0,1:T(8,128)} copy(f32[16,8]{1,0:T(8,128)S(1)} %get-tuple-element.5) | data formatting | bytes 1024 | tf_op jit(solution)/shard_map/pallas_call | solution.py:407
  52.7 0.6 %copy.14 = bf16[16,2048]{1,0:T(8,128)(2,1)} copy(bf16[16,2048]{1,0:T(8,128)(2,1)S(1)} %get-tuple-element.9) | data formatting | bytes 131072
  53.3 0.6 %copy.15 = bf16[16,2048]{1,0:T(8,128)(2,1)} copy(bf16[16,2048]{1,0:T(8,128)(2,1)S(1)} %get-tuple-element.10) | data formatting | bytes 131072
Async XLA Ops:
  2.1 1.9 %copy-start = (bf16[1,2048,768]{2,1,0:T(8,128)(2,1)S(1)}, bf16[1,2048,768]{2,1,0:T(8,128)(2,1)}, u32[]{:S(2)}) copy-start(bf16[1,2048,768]{2,1,0:T(8,128)(2,1)} %gate_up_hbm.1) | copy-start | bytes 9437188
  4.0 1.4 %copy-start.1 = (bf16[1,384,2048]{2,1,0:T(8,128)(2,1)S(1)}, bf16[1,384,2048]{2,1,0:T(8,128)(2,1)}, u32[]{:S(2)}) copy-start(bf16[1,384,2048]{2,1,0:T(8,128)(2,1)} %down_hbm.1) | copy-start | bytes 4718596
  5.4 0.8 %copy-start.2 = (bf16[16,2048]{1,0:T(8,128)(2,1)S(1)}, bf16[16,2048]{1,0:T(8,128)(2,1)}, u32[]{:S(2)}) copy-start(bf16[16,2048]{1,0:T(8,128)(2,1)} %tok_ref.1) | copy-start | bytes 196612
  6.3 0.8 %copy-start.3 = (bf16[16,2048]{1,0:T(8,128)(2,1)S(1)}, bf16[16,2048]{1,0:T(8,128)(2,1)}, u32[]{:S(2)}) copy-start(bf16[16,2048]{1,0:T(8,128)(2,1)} %cot_ref.1) | copy-start | bytes 196612

commit v2 on v1

--- a/solution.py
+++ b/solution.py
@@ -118,15 +118,17 @@
 
 def dense_kernel(
     n,
-    tok_ref,
-    cot_ref,
-    ids_ref,
-    comb_ref,
+    tok_hbm,
+    cot_hbm,
+    ids_hbm,
+    comb_hbm,
     gate_up_hbm,
     down_hbm,
     mixed_ref,
     grad_ref,
     gcomb_ref,
+    ids_t,
+    comb_t,
     wgu,
     wd,
     xs,
@@ -147,6 +149,7 @@
     zr_m,
     zr_b,
     w_sem,
+    nd_send,
     ag_send,
     ag_recv,
     core_send,
@@ -156,8 +159,8 @@
     z_send,
     z_recv,
 ):
-    tok, width = tok_ref.shape
-    top = ids_ref.shape[1]
+    tok, width = tok_hbm.shape
+    top = ids_hbm.shape[0]
     ff = wd.shape[0]
     z = lax.axis_index("node")
     local = lax.axis_index("local")
@@ -170,8 +173,16 @@
     partner = {"local": (1 - x) * 2 + c}
     sibling = {"local": x * 2 + 1 - c}
 
-    def zdev(d):
-        return {"node": lax.rem(z + d, n)}
+    reach = jnp.minimum(z, n - 1 - z)
+    toward = jnp.where(z < n - 1 - z, 1, -1)
+    near = []
+    for s in range(1, n):
+        turn = (s + 1) // 2 * (1 if s % 2 else -1)
+        near.append(z + toward * jnp.where(s <= 2 * reach, turn, s - reach))
+    far = near[::-1]
+
+    def zdev(zz):
+        return {"node": zz}
 
     def column(xx, cc):
         return pl.multiple_of((xx * 2 + cc) * quarter, quarter)
@@ -179,29 +190,37 @@
     def rows(xx, cc, zz):
         return pl.ds(pl.multiple_of(((xx * 2 + cc) * n + zz) * tok, tok), tok)
 
+    mine = rows(x, c, z)
+    load_own = [
+        pltpu.make_async_copy(ids_hbm, ids_t, w_sem.at[2]),
+        pltpu.make_async_copy(comb_hbm, comb_t, w_sem.at[3]),
+        pltpu.make_async_copy(tok_hbm, xs.at[mine, pl.ds(0, width)], w_sem.at[4]),
+        pltpu.make_async_copy(cot_hbm, cs.at[mine], w_sem.at[5]),
+    ]
+    for copy in load_own:
+        copy.start()
     load_gu = pltpu.make_async_copy(gate_up_hbm.at[0], wgu, w_sem.at[0])
     load_d = pltpu.make_async_copy(down_hbm.at[0], wd, w_sem.at[1])
     load_gu.start()
     load_d.start()
 
     barrier = pltpu.get_barrier_semaphore()
-    for d in range(1, n):
-        pl.semaphore_signal(barrier, inc=1, device_id=zdev(d), device_id_type=MESH)
+    for zz in near:
+        pl.semaphore_signal(barrier, inc=1, device_id=zdev(zz), device_id_type=MESH)
     pl.semaphore_signal(barrier, inc=1, device_id=partner, device_id_type=MESH)
     pl.semaphore_signal(barrier, inc=1, device_id=sibling, device_id_type=MESH)
 
-    mine = rows(x, c, z)
+    for copy in load_own:
+        copy.wait()
     lane = lax.broadcasted_iota(jnp.int32, (tok, LANES), 1)
     lane_expert = jnp.where(lane < experts, lane, lane - experts)
-    ids = ids_ref[...]
-    comb = comb_ref[...]
+    ids = ids_t[...].T
+    comb = comb_t[...].T
     weight = jnp.zeros((tok, LANES), F32)
     for k in range(top):
         weight = weight + jnp.where(ids[:, k : k + 1] == lane_expert, comb[:, k : k + 1], 0.0)
     coarse = weight.astype(BF16).astype(F32)
-    xs[mine, :width] = tok_ref[...]
     xs[mine, width:] = jnp.where(lane < experts, coarse, weight - coarse).astype(BF16)
-    cs[mine, :] = cot_ref[...]
     pl.semaphore_wait(barrier, n + 1)
 
     sends = []
@@ -223,40 +242,37 @@
 
     bufs = (xs, cs)
 
-    def gather_go(t, role, d, where, device):
-        go(bufs[t].at[where], bufs[t].at[where], ag_send.at[t, role, d], ag_recv.at[t, role, d], device)
-
-    def gather_wait(t, role, d, where):
+    def gather_go(t, role, zz, where, device):
+        go(bufs[t].at[where], bufs[t].at[where], ag_send.at[t, role, zz], ag_recv.at[t, role, zz], device)
+
+    def gather_wait(t, role, zz, where):
         remote(
-            bufs[t].at[where], bufs[t].at[where], ag_send.at[t, role, d], ag_recv.at[t, role, d], sibling
+            bufs[t].at[where], bufs[t].at[where], ag_send.at[t, role, zz], ag_recv.at[t, role, zz], sibling
         ).wait_recv()
 
-    def back_by(d):
-        return lax.rem(z + n - d, n)
-
     for t in range(2):
-        gather_go(t, 1, 0, mine, partner)
-        for d in range(1, n):
-            gather_go(t, 0, d, mine, zdev(d))
-        gather_go(t, 2, 0, mine, sibling)
-
-    def pass_z(t):
-        for d in range(1, n):
-            where = rows(x, c, back_by(d))
-            gather_wait(t, 0, d, where)
-            gather_go(t, 1, d, where, partner)
-            gather_go(t, 2, d, where, sibling)
+        gather_go(t, 1, z, mine, partner)
+        for i, zz in enumerate(near):
+            go(bufs[t].at[mine], bufs[t].at[mine], nd_send.at[t, i], ag_recv.at[t, 0, z], zdev(zz))
+        gather_go(t, 2, z, mine, sibling)
+
+    def pass_z(t, places):
+        for zz in places:
+            where = rows(x, c, zz)
+            gather_wait(t, 0, zz, where)
+            gather_go(t, 1, zz, where, partner)
+            gather_go(t, 2, zz, where, sibling)
 
     def pass_x(t):
-        for d in range(n):
-            where = rows(1 - x, c, back_by(d))
-            gather_wait(t, 1, d, where)
-            gather_go(t, 3, d, where, sibling)
+        for zz in [z] + near:
+            where = rows(1 - x, c, zz)
+            gather_wait(t, 1, zz, where)
+            gather_go(t, 3, zz, where, sibling)
 
     def await_sibling(t, other):
-        for d in range(n):
-            where = rows(1 - x if other else x, 1 - c, back_by(d))
-            gather_wait(t, 3 if other else 2, d, where)
+        for zz in [z] + near:
+            where = rows(1 - x if other else x, 1 - c, zz)
+            gather_wait(t, 3 if other else 2, zz, where)
 
     tile = 512 if width % 512 == 0 else width
     wide_lane = lax.broadcasted_iota(jnp.int32, (half, LANES), 1)
@@ -321,64 +337,64 @@
     def core_wait(t, other):
         remote(*core_copy(t, other)).wait_recv()
 
-    def core_rows(d):
-        return pl.ds(pl.multiple_of(lax.rem(z + d, n) * tok, tok), tok)
-
-    def x_copy(t, d):
-        return (to_x[t].at[d], from_x[t].at[d], x_send.at[t, d], x_recv.at[t, d], partner)
-
-    def z_copy(t, d):
-        return (to_z[t].at[d], from_z[t].at[d], z_send.at[t, d], z_recv.at[t, d], zdev(d))
-
-    order = [d for d in range(1, n)] + [0]
+    def core_rows(zz):
+        return pl.ds(pl.multiple_of(zz * tok, tok), tok)
+
+    def x_copy(t, zz):
+        return (to_x[t].at[zz], from_x[t].at[zz], x_send.at[t, zz], x_recv.at[t, zz], partner)
+
+    order = far + [z]
 
     def send_x(t):
         core_wait(t, True)
-        for d in order:
-            own = parts[t][rows(1 - x, c, lax.rem(z + d, n)), :].astype(F32)
-            to_x[t][d] = (own + from_core[t][1, core_rows(d), :].astype(F32)).astype(BF16)
-            go(*x_copy(t, d))
-
-    def joined(t, d):
-        own = parts[t][rows(x, c, lax.rem(z + d, n)), :].astype(F32)
-        return own + from_core[t][0, core_rows(d), :].astype(F32) + from_x[t][d].astype(F32)
+        for zz in order:
+            own = parts[t][rows(1 - x, c, zz), :].astype(F32)
+            to_x[t][zz] = (own + from_core[t][1, core_rows(zz), :].astype(F32)).astype(BF16)
+            go(*x_copy(t, zz))
+
+    def joined(t, zz):
+        own = parts[t][rows(x, c, zz), :].astype(F32)
+        return own + from_core[t][0, core_rows(zz), :].astype(F32) + from_x[t][zz].astype(F32)
 
     def send_z(t):
         core_wait(t, False)
-        for d in order:
-            remote(*x_copy(t, d)).wait_recv()
-            if d > 0:
-                to_z[t][d] = joined(t, d).astype(BF16)
-                go(*z_copy(t, d))
+        for zz in far:
+            remote(*x_copy(t, zz)).wait_recv()
+            to_z[t][zz] = joined(t, zz).astype(BF16)
+            go(to_z[t].at[zz], from_z[t].at[z], z_send.at[t, zz], z_recv.at[t, z], zdev(zz))
 
     def finish(t):
-        total = joined(t, 0)
-        for d in range(1, n):
-            remote(*z_copy(t, d)).wait_recv()
-            total = total + from_z[t][d].astype(F32)
+        remote(*x_copy(t, z)).wait_recv()
+        total = joined(t, z)
+        for zz in near:
+            remote(
+                to_z[t].at[zz], from_z[t].at[zz], z_send.at[t, zz], z_recv.at[t, zz], zdev(zz)
+            ).wait_recv()
+            total = total + from_z[t][zz].astype(F32)
         return total
 
-    pass_z(0)
-    pass_z(1)
+    pass_z(0, near)
     load_gu.wait()
     load_d.wait()
-    pass_x(0)
     await_sibling(0, False)
     forward(False)
     core_go(0, False)
+    pass_x(0)
+    pass_z(1, near[:-1])
     await_sibling(0, True)
     forward(True)
     core_go(0, True)
+    pass_z(1, near[-1:])
+    send_x(0)
     await_sibling(1, False)
     backward(False)
     core_go(1, False)
-    send_x(0)
     pass_x(1)
     await_sibling(1, True)
     backward(True)
     core_go(1, True)
+    send_z(0)
     send_x(1)
-    send_z(0)
     mixed_ref[...] = finish(0).astype(mixed_ref.dtype)
     send_z(1)
     total = finish(1)
@@ -389,7 +405,7 @@
     for k in range(top):
         value = jnp.sum(jnp.where(ids[:, k : k + 1] == lane_expert, dots, 0.0), axis=1, keepdims=True)
         picked = picked + jnp.where(place == k, value, 0.0)
-    gcomb_ref[...] = picked
+    gcomb_ref[...] = picked.T
     for copy in sends:
         copy.wait_send()
 
@@ -404,16 +420,18 @@
     vmem = pl.BlockSpec(memory_space=pltpu.VMEM)
     hbm = pl.BlockSpec(memory_space=pl.ANY)
     dma = pltpu.SemaphoreType.DMA
-    return pl.pallas_call(
+    mixed, grads, dots = pl.pallas_call(
         functools.partial(dense_kernel, n),
         out_shape=(
             jax.ShapeDtypeStruct((tok, width), BF16),
             jax.ShapeDtypeStruct((tok, width), BF16),
-            jax.ShapeDtypeStruct((tok, top), F32),
+            jax.ShapeDtypeStruct((top, tok), F32),
         ),
-        in_specs=[vmem, vmem, vmem, vmem, hbm, hbm],
+        in_specs=[hbm] * 6,
         out_specs=(vmem, vmem, vmem),
         scratch_shapes=[
+            pltpu.VMEM((top, tok), jnp.int32),
+            pltpu.VMEM((top, tok), F32),
             pltpu.VMEM((width, 2 * ff), BF16),
             pltpu.VMEM((ff, width), BF16),
             pltpu.VMEM((total, wide), BF16),
@@ -433,7 +451,8 @@
             pltpu.VMEM((n, tok, wide), BF16),
             pltpu.VMEM((n, tok, width), BF16),
             pltpu.VMEM((n, tok, wide), BF16),
-            dma((2,)),
+            dma((6,)),
+            dma((2, n)),
             dma((2, 4, n)),
             dma((2, 4, n)),
             dma((2, 2)),
@@ -444,9 +463,10 @@
             dma((2, n)),
         ],
         compiler_params=pltpu.CompilerParams(
-            collective_id=0, has_side_effects=True, vmem_limit_bytes=40 * 1024 * 1024
+            collective_id=0, has_side_effects=True, vmem_limit_bytes=62 * 1024 * 1024
         ),
-    )(tokens, cotangent, expert_ids, combine, w_gate_up, w_down)
+    )(tokens, cotangent, expert_ids.T, combine.T, w_gate_up, w_down)
+    return mixed, grads, dots.T
 
 
 def choose_plan(tokens, cotangent, expert_ids, combine, w_gate_up, w_down):

time: 54.3 us -> 48.5 us (0.89)
  local copies, waits for them, and re-layouts: 8.41 us -> 4.22 us
  Pallas kernels: 44.9 us -> 43.4 us
    unnamed x12 -> x3, local copies, waits for them, and re-layouts: 7.75 us -> 4.22 us
    pallas_call x1, Pallas kernels: 44.9 us -> 43.4 us  [dense_plan(): pl.pallas_call(functools.partial(dense_kernel, n), out_shape=(jax.ShapeDt...]
    pallas_call x1 -> x0, local copies, waits for them, and re-layouts: 0.66 us -> none  [dense_plan(): pl.pallas_call(functools.partial(dense_kernel, n), out_shape=(jax.ShapeDt...]
where the time goes in v2:
time: 48.5 us; the launch traced here: 48.2 us
  Pallas kernels  43.4 us (89%)
  local copies, waits for them, and re-layouts  4.22 us (9%)
  between operations  0.64 us (1%)
    pallas_call x1, Pallas kernels, dense_plan(): pl.pallas_call(functools.partial(dense_kernel, n), out_shape=(jax.ShapeDt...  43.4 us
    unnamed x3, local copies, waits for them, and re-layouts  4.22 us

profile of v2, /device:TPU:0, one launch (start us, length us, event | category | flops | bytes accessed | tf_op | source)
XLA Modules:
  0.0 48.2 jit_solution(5099290608210929760)
XLA Ops:
  0.6 43.4 %shard_map.85 = (bf16[16,2048]{1,0:T(8,128)(2,1)}, bf16[16,2048]{1,0:T(8,128)(2,1)}, f32[8,16]{1,0:T(8,128)}) custom-call(bf16[16,2048]{1,0:T(8,128)(2,1)} %tok_hbm.1, bf16[16,2048]{1,0:T(8,128)(2,1)} %cot_hbm.1, s32[8,16]{1,0:T(8,128)} %bitcast.3, f32[8,16]{1,0:T(8,128)} %bitcast.4, bf16[1,2048,768]{2,1,0:T(8,128)(2,1)} %gate_up_hbm.1, ...), custom_call_target="tpu_custom_call" | custom-call | tf_op jit(solution)/shard_map/pallas_call | solution.py:423
  44.0 1.5 %copy.12 = bf16[16,2048]{1,0:T(8,128)(2,1)} copy(bf16[16,2048]{1,0:T(8,128)(2,1)} %get-tuple-element.12) | data formatting | bytes 131072
  45.5 1.5 %copy.13 = bf16[16,2048]{1,0:T(8,128)(2,1)} copy(bf16[16,2048]{1,0:T(8,128)(2,1)} %get-tuple-element.13) | data formatting | bytes 131072
  46.9 1.3 %copy.14 = f32[16,8]{0,1:T(8,128)} copy(f32[16,8]{0,1:T(8,128)} %bitcast.5) | data formatting | bytes 1024

commit v3 on v2

--- a/solution.py
+++ b/solution.py
@@ -224,6 +224,7 @@
     pl.semaphore_wait(barrier, n + 1)
 
     sends = []
+    maybe = []
 
     def remote(src, dst, send_sem, recv_sem, device):
         return pltpu.make_async_remote_copy(
@@ -250,18 +251,35 @@
             bufs[t].at[where], bufs[t].at[where], ag_send.at[t, role, zz], ag_recv.at[t, role, zz], sibling
         ).wait_recv()
 
-    for t in range(2):
+    def inside(zz):
+        return (zz >= 0) & (zz < n)
+
+    def go_if(cond, *args):
+        copy = remote(*args)
+        pl.when(cond)(copy.start)
+        maybe.append((cond, copy))
+
+    def own_go(t):
+        for i, to in enumerate((z - 1, z + 1)):
+            device = zdev(jnp.clip(to, 0, n - 1))
+            block = bufs[t].at[mine]
+            go_if(inside(to), block, block, nd_send.at[t, i], ag_recv.at[t, 0, z], device)
         gather_go(t, 1, z, mine, partner)
-        for i, zz in enumerate(near):
-            go(bufs[t].at[mine], bufs[t].at[mine], nd_send.at[t, i], ag_recv.at[t, 0, z], zdev(zz))
         gather_go(t, 2, z, mine, sibling)
 
-    def pass_z(t, places):
-        for zz in places:
+    def pass_z(t, s):
+        for side in (-1, 1):
+            here = inside(z + side * s)
+            zz = jnp.clip(z + side * s, 0, n - 1)
+            to = z - side
             where = rows(x, c, zz)
-            gather_wait(t, 0, zz, where)
-            gather_go(t, 1, zz, where, partner)
-            gather_go(t, 2, zz, where, sibling)
+            block = bufs[t].at[where]
+            pl.when(here)(functools.partial(gather_wait, t, 0, zz, where))
+            if s < n - 1:
+                device = zdev(jnp.clip(to, 0, n - 1))
+                go_if(here & inside(to), block, block, ag_send.at[t, 0, zz], ag_recv.at[t, 0, zz], device)
+            go_if(here, block, block, ag_send.at[t, 1, zz], ag_recv.at[t, 1, zz], partner)
+            go_if(here, block, block, ag_send.at[t, 2, zz], ag_recv.at[t, 2, zz], sibling)
 
     def pass_x(t):
         for zz in [z] + near:
@@ -373,18 +391,24 @@
             total = total + from_z[t][zz].astype(F32)
         return total
 
-    pass_z(0, near)
+    own_go(0)
+    for s in range(1, n):
+        pass_z(0, s)
+        if s == 1:
+            own_go(1)
+        if s == 2:
+            pass_z(1, 1)
     load_gu.wait()
     load_d.wait()
     await_sibling(0, False)
     forward(False)
     core_go(0, False)
+    for s in range(min(2, n - 1), n):
+        pass_z(1, s)
     pass_x(0)
-    pass_z(1, near[:-1])
     await_sibling(0, True)
     forward(True)
     core_go(0, True)
-    pass_z(1, near[-1:])
     send_x(0)
     await_sibling(1, False)
     backward(False)
@@ -408,6 +432,8 @@
     gcomb_ref[...] = picked.T
     for copy in sends:
         copy.wait_send()
+    for cond, copy in maybe:
+        pl.when(cond)(copy.wait_send)
 
 
 def dense_plan(tokens, cotangent, expert_ids, combine, w_gate_up, w_down):

time: 48.5 us -> 47.8 us (0.986)
  Pallas kernels: 43.4 us -> 42.7 us
    pallas_call x1, Pallas kernels: 43.4 us -> 42.7 us  [dense_plan(): pl.pallas_call(functools.partial(dense_kernel, n), out_shape=(jax.ShapeDt...]
where the time goes in v3:
time: 47.8 us; the launch traced here: 47.6 us
  Pallas kernels  42.7 us (89%)
  local copies, waits for them, and re-layouts  4.22 us (9%)
  between operations  0.64 us (1%)
    pallas_call x1, Pallas kernels, dense_plan(): pl.pallas_call(functools.partial(dense_kernel, n), out_shape=(jax.ShapeDt...  42.7 us
    unnamed x3, local copies, waits for them, and re-layouts  4.22 us

profile of v3, /device:TPU:0, one launch (start us, length us, event | category | flops | bytes accessed | tf_op | source)
XLA Modules:
  0.0 47.6 jit_solution(10310034526935104478)
XLA Ops:
  0.6 42.7 %shard_map.85 = (bf16[16,2048]{1,0:T(8,128)(2,1)}, bf16[16,2048]{1,0:T(8,128)(2,1)}, f32[8,16]{1,0:T(8,128)}) custom-call(bf16[16,2048]{1,0:T(8,128)(2,1)} %tok_hbm.1, bf16[16,2048]{1,0:T(8,128)(2,1)} %cot_hbm.1, s32[8,16]{1,0:T(8,128)} %bitcast.3, f32[8,16]{1,0:T(8,128)} %bitcast.4, bf16[1,2048,768]{2,1,0:T(8,128)(2,1)} %gate_up_hbm.1, ...), custom_call_target="tpu_custom_call" | custom-call | tf_op jit(solution)/shard_map/pallas_call | solution.py:449
  43.3 1.5 %copy.12 = bf16[16,2048]{1,0:T(8,128)(2,1)} copy(bf16[16,2048]{1,0:T(8,128)(2,1)} %get-tuple-element.12) | data formatting | bytes 131072
  44.8 1.5 %copy.13 = bf16[16,2048]{1,0:T(8,128)(2,1)} copy(bf16[16,2048]{1,0:T(8,128)(2,1)} %get-tuple-element.13) | data formatting | bytes 131072
  46.3 1.3 %copy.14 = f32[16,8]{0,1:T(8,128)} copy(f32[16,8]{0,1:T(8,128)} %bitcast.5) | data formatting | bytes 1024

commit v4 on v3

--- a/solution.py
+++ b/solution.py
@@ -138,6 +138,7 @@
     gate_s,
     up_s,
     hid_s,
+    pair_s,
     cr_m,
     cr_b,
     xs_m,
@@ -293,52 +294,53 @@
             gather_wait(t, 3 if other else 2, zz, where)
 
     tile = 512 if width % 512 == 0 else width
-    wide_lane = lax.broadcasted_iota(jnp.int32, (half, LANES), 1)
-
-    def chunk(other):
-        return pl.ds(pl.multiple_of((1 - x if other else x) * half, half), half)
-
-    def my_weight(r):
-        block = xs[r, width:].astype(F32)
+    total_rows = 2 * half
+    wide_lane = lax.broadcasted_iota(jnp.int32, (total_rows, LANES), 1)
+
+    def my_weight():
+        block = xs[:, width:].astype(F32)
         chosen = (wide_lane == me) | (wide_lane == me + experts)
         return jnp.sum(jnp.where(chosen, block, 0.0), axis=1, keepdims=True)
 
-    def forward(other):
-        r = chunk(other)
-        projected = jnp.dot(xs[r, :width], wgu[...], preferred_element_type=F32)
+    def forward():
+        projected = jnp.dot(xs[:, :width], wgu[...], preferred_element_type=F32)
         gate = projected[:, :ff]
         upward = projected[:, ff:]
         hidden = (gate * jax.nn.sigmoid(gate) * upward).astype(BF16)
-        gate_s[r, :] = gate
-        up_s[r, :] = upward
-        hid_s[r, :] = hidden
-        weight = my_weight(r)
-        for j in range(width // tile):
-            cols = slice(j * tile, (j + 1) * tile)
-            out = jnp.dot(hidden, wd[:, cols], preferred_element_type=F32)
-            pm[r, cols] = (out * weight).astype(BF16)
+        gate_s[...] = gate
+        up_s[...] = upward
+        hid_s[...] = hidden
+        weight = my_weight()
+
+        @pl.loop(0, width // tile)
+        def _(j):
+            cols = pl.ds(pl.multiple_of(j * tile, tile), tile)
+            out = jnp.dot(hid_s[...], wd[:, cols], preferred_element_type=F32)
+            pm[:, cols] = (out * weight).astype(BF16)
 
     across = (((1,), (1,)), ((), ()))
 
-    def backward(other):
-        r = chunk(other)
-        plain = lax.dot_general(cs[r, :], wd[...], across, preferred_element_type=F32)
-        gate = gate_s[r, :]
-        upward = up_s[r, :]
-        grads = plain * my_weight(r)
+    def backward():
+        plain = lax.dot_general(cs[...], wd[...], across, preferred_element_type=F32)
+        gate = gate_s[...]
+        upward = up_s[...]
+        grads = plain * my_weight()
         sig = jax.nn.sigmoid(gate)
         grad_gate = grads * upward * sig * (1.0 + gate * (1.0 - sig))
         grad_up = grads * gate * sig
-        dots = jnp.sum(plain * hid_s[r, :].astype(F32), axis=1, keepdims=True)
+        dots = jnp.sum(plain * hid_s[...].astype(F32), axis=1, keepdims=True)
         coarse = dots.astype(BF16).astype(F32)
-        pb[r, width:] = jnp.where(
+        pb[:, width:] = jnp.where(
             wide_lane == me, coarse, jnp.where(wide_lane == me + experts, dots - coarse, 0.0)
         ).astype(BF16)
-        paired = jnp.concatenate([grad_gate, grad_up], axis=1).astype(BF16)
-        for j in range(width // tile):
-            cols = slice(j * tile, (j + 1) * tile)
-            back = lax.dot_general(paired, wgu[cols, :], across, preferred_element_type=F32)
-            pb[r, cols] = back.astype(BF16)
+        pair_s[:, :ff] = grad_gate.astype(BF16)
+        pair_s[:, ff:] = grad_up.astype(BF16)
+
+        @pl.loop(0, width // tile)
+        def _(j):
+            cols = pl.ds(pl.multiple_of(j * tile, tile), tile)
+            back = lax.dot_general(pair_s[...], wgu[cols, :], across, preferred_element_type=F32)
+            pb[:, cols] = back.astype(BF16)
 
     parts, from_core = (pm, pb), (cr_m, cr_b)
     to_x, from_x = (xs_m, xs_b), (xr_m, xr_b)
@@ -398,25 +400,23 @@
             own_go(1)
         if s == 2:
             pass_z(1, 1)
+    pass_x(0)
+    for s in range(min(2, n - 1), n):
+        pass_z(1, s)
     load_gu.wait()
     load_d.wait()
     await_sibling(0, False)
-    forward(False)
+    await_sibling(0, True)
+    forward()
+    core_go(0, True)
     core_go(0, False)
-    for s in range(min(2, n - 1), n):
-        pass_z(1, s)
-    pass_x(0)
-    await_sibling(0, True)
-    forward(True)
-    core_go(0, True)
+    pass_x(1)
     send_x(0)
     await_sibling(1, False)
-    backward(False)
+    await_sibling(1, True)
+    backward()
+    core_go(1, True)
     core_go(1, False)
-    pass_x(1)
-    await_sibling(1, True)
-    backward(True)
-    core_go(1, True)
     send_z(0)
     send_x(1)
     mixed_ref[...] = finish(0).astype(mixed_ref.dtype)
@@ -467,6 +467,7 @@
             pltpu.VMEM((total, ff), F32),
             pltpu.VMEM((total, ff), F32),
             pltpu.VMEM((total, ff), BF16),
+            pltpu.VMEM((total, 2 * ff), BF16),
             pltpu.VMEM((2, n * tok, width), BF16),
             pltpu.VMEM((2, n * tok, wide), BF16),
             pltpu.VMEM((n, tok, width), BF16),

time: 47.8 us -> 46.2 us (0.967)
  Pallas kernels: 42.7 us -> 41.1 us
    pallas_call x1, Pallas kernels: 42.7 us -> 41.1 us  [dense_plan(): pl.pallas_call(functools.partial(dense_kernel, n), out_shape=(jax.ShapeDt...]
where the time goes in v4:
time: 46.2 us; the launch traced here: 45.9 us
  Pallas kernels  41.1 us (89%)
  local copies, waits for them, and re-layouts  4.22 us (9%)
  between operations  0.64 us (1%)
    pallas_call x1, Pallas kernels, dense_plan(): pl.pallas_call(functools.partial(dense_kernel, n), out_shape=(jax.ShapeDt...  41.1 us
    unnamed x3, local copies, waits for them, and re-layouts  4.22 us

profile of v4, /device:TPU:0, one launch (start us, length us, event | category | flops | bytes accessed | tf_op | source)
XLA Modules:
  0.0 45.9 jit_solution(9812434229997758681)
XLA Ops:
  0.6 41.1 %shard_map.85 = (bf16[16,2048]{1,0:T(8,128)(2,1)}, bf16[16,2048]{1,0:T(8,128)(2,1)}, f32[8,16]{1,0:T(8,128)}) custom-call(bf16[16,2048]{1,0:T(8,128)(2,1)} %tok_hbm.1, bf16[16,2048]{1,0:T(8,128)(2,1)} %cot_hbm.1, s32[8,16]{1,0:T(8,128)} %bitcast.3, f32[8,16]{1,0:T(8,128)} %bitcast.4, bf16[1,2048,768]{2,1,0:T(8,128)(2,1)} %gate_up_hbm.1, ...), custom_call_target="tpu_custom_call" | custom-call | tf_op jit(solution)/shard_map/pallas_call | solution.py:449
  41.7 1.5 %copy.12 = bf16[16,2048]{1,0:T(8,128)(2,1)} copy(bf16[16,2048]{1,0:T(8,128)(2,1)} %get-tuple-element.12) | data formatting | bytes 131072
  43.2 1.5 %copy.13 = bf16[16,2048]{1,0:T(8,128)(2,1)} copy(bf16[16,2048]{1,0:T(8,128)(2,1)} %get-tuple-element.13) | data formatting | bytes 131072
  44.6 1.3 %copy.14 = f32[16,8]{0,1:T(8,128)} copy(f32[16,8]{0,1:T(8,128)} %bitcast.5) | data formatting | bytes 1024

commit v5 on v4

--- a/solution.py
+++ b/solution.py
@@ -118,6 +118,7 @@
 
 def dense_kernel(
     n,
+    tiles,
     tok_hbm,
     cot_hbm,
     ids_hbm,
@@ -133,22 +134,16 @@
     wd,
     xs,
     cs,
-    pm,
-    pb,
     gate_s,
     up_s,
     hid_s,
     pair_s,
-    cr_m,
-    cr_b,
-    xs_m,
-    xs_b,
-    xr_m,
-    xr_b,
-    zs_m,
-    zs_b,
-    zr_m,
-    zr_b,
+    parts,
+    from_core,
+    to_x,
+    from_x,
+    to_z,
+    from_z,
     w_sem,
     nd_send,
     ag_send,
@@ -170,6 +165,7 @@
     me = z * 4 + local
     half = 2 * n * tok
     quarter = n * tok
+    tile = width // tiles
 
     partner = {"local": (1 - x) * 2 + c}
     sibling = {"local": x * 2 + 1 - c}
@@ -260,13 +256,19 @@
         pl.when(cond)(copy.start)
         maybe.append((cond, copy))
 
-    def own_go(t):
+    def own_go_z(t):
         for i, to in enumerate((z - 1, z + 1)):
             device = zdev(jnp.clip(to, 0, n - 1))
             block = bufs[t].at[mine]
             go_if(inside(to), block, block, nd_send.at[t, i], ag_recv.at[t, 0, z], device)
+
+    def own_go_near(t):
         gather_go(t, 1, z, mine, partner)
         gather_go(t, 2, z, mine, sibling)
+
+    def own_go(t):
+        own_go_near(t)
+        own_go_z(t)
 
     def pass_z(t, s):
         for side in (-1, 1):
@@ -293,7 +295,6 @@
             where = rows(1 - x if other else x, 1 - c, zz)
             gather_wait(t, 3 if other else 2, zz, where)
 
-    tile = 512 if width % 512 == 0 else width
     total_rows = 2 * half
     wide_lane = lax.broadcasted_iota(jnp.int32, (total_rows, LANES), 1)
 
@@ -302,133 +303,127 @@
         chosen = (wide_lane == me) | (wide_lane == me + experts)
         return jnp.sum(jnp.where(chosen, block, 0.0), axis=1, keepdims=True)
 
-    def forward():
+    def forward_hidden():
         projected = jnp.dot(xs[:, :width], wgu[...], preferred_element_type=F32)
         gate = projected[:, :ff]
         upward = projected[:, ff:]
-        hidden = (gate * jax.nn.sigmoid(gate) * upward).astype(BF16)
         gate_s[...] = gate
         up_s[...] = upward
-        hid_s[...] = hidden
-        weight = my_weight()
-
-        @pl.loop(0, width // tile)
-        def _(j):
-            cols = pl.ds(pl.multiple_of(j * tile, tile), tile)
-            out = jnp.dot(hid_s[...], wd[:, cols], preferred_element_type=F32)
-            pm[:, cols] = (out * weight).astype(BF16)
+        hid_s[...] = (gate * jax.nn.sigmoid(gate) * upward).astype(BF16)
+
+    def forward_tile(j, weight):
+        cols = slice(j * tile, (j + 1) * tile)
+        out = jnp.dot(hid_s[...], wd[:, cols], preferred_element_type=F32)
+        parts[j][...] = (out * weight).astype(BF16)
 
     across = (((1,), (1,)), ((), ()))
 
-    def backward():
+    def backward_hidden(weight):
         plain = lax.dot_general(cs[...], wd[...], across, preferred_element_type=F32)
         gate = gate_s[...]
         upward = up_s[...]
-        grads = plain * my_weight()
+        grads = plain * weight
         sig = jax.nn.sigmoid(gate)
         grad_gate = grads * upward * sig * (1.0 + gate * (1.0 - sig))
         grad_up = grads * gate * sig
         dots = jnp.sum(plain * hid_s[...].astype(F32), axis=1, keepdims=True)
         coarse = dots.astype(BF16).astype(F32)
-        pb[:, width:] = jnp.where(
+        parts[tiles][...] = jnp.where(
             wide_lane == me, coarse, jnp.where(wide_lane == me + experts, dots - coarse, 0.0)
         ).astype(BF16)
         pair_s[:, :ff] = grad_gate.astype(BF16)
         pair_s[:, ff:] = grad_up.astype(BF16)
 
-        @pl.loop(0, width // tile)
-        def _(j):
-            cols = pl.ds(pl.multiple_of(j * tile, tile), tile)
-            back = lax.dot_general(pair_s[...], wgu[cols, :], across, preferred_element_type=F32)
-            pb[:, cols] = back.astype(BF16)
-
-    parts, from_core = (pm, pb), (cr_m, cr_b)
-    to_x, from_x = (xs_m, xs_b), (xr_m, xr_b)
-    to_z, from_z = (zs_m, zs_b), (zr_m, zr_b)
-
-    def core_copy(t, other):
-        src = parts[t].at[pl.ds(column(1 - x if other else x, 1 - c), quarter)]
+    def backward_tile(j):
+        cols = slice(j * tile, (j + 1) * tile)
+        back = lax.dot_general(pair_s[...], wgu[cols, :], across, preferred_element_type=F32)
+        parts[tiles + 1 + j][...] = back.astype(BF16)
+
+    def core_copy(i, other):
+        src = parts[i].at[pl.ds(column(1 - x if other else x, 1 - c), quarter)]
         q = 1 if other else 0
-        return (src, from_core[t].at[q], core_send.at[t, q], core_recv.at[t, q], sibling)
-
-    def core_go(t, other):
-        go(*core_copy(t, other))
-
-    def core_wait(t, other):
-        remote(*core_copy(t, other)).wait_recv()
-
-    def core_rows(zz):
+        return (src, from_core[i].at[q], core_send.at[i, q], core_recv.at[i, q], sibling)
+
+    def core_go(i):
+        go(*core_copy(i, True))
+        go(*core_copy(i, False))
+
+    def x_copy(i):
+        return (to_x[i], from_x[i], x_send.at[i], x_recv.at[i], partner)
+
+    def x_stage(i):
+        remote(*core_copy(i, True)).wait_recv()
+        own = parts[i][pl.ds(column(1 - x, c), quarter), :].astype(F32)
+        to_x[i][...] = (own + from_core[i][1].astype(F32)).astype(BF16)
+        go(*x_copy(i))
+
+    def place(zz):
         return pl.ds(pl.multiple_of(zz * tok, tok), tok)
 
-    def x_copy(t, zz):
-        return (to_x[t].at[zz], from_x[t].at[zz], x_send.at[t, zz], x_recv.at[t, zz], partner)
-
-    order = far + [z]
-
-    def send_x(t):
-        core_wait(t, True)
-        for zz in order:
-            own = parts[t][rows(1 - x, c, zz), :].astype(F32)
-            to_x[t][zz] = (own + from_core[t][1, core_rows(zz), :].astype(F32)).astype(BF16)
-            go(*x_copy(t, zz))
-
-    def joined(t, zz):
-        own = parts[t][rows(x, c, zz), :].astype(F32)
-        return own + from_core[t][0, core_rows(zz), :].astype(F32) + from_x[t][zz].astype(F32)
-
-    def send_z(t):
-        core_wait(t, False)
+    def z_stage(i):
+        remote(*core_copy(i, False)).wait_recv()
+        remote(*x_copy(i)).wait_recv()
+        own = parts[i][pl.ds(column(x, c), quarter), :].astype(F32)
+        to_z[i][...] = (own + from_core[i][0].astype(F32) + from_x[i][...].astype(F32)).astype(BF16)
         for zz in far:
-            remote(*x_copy(t, zz)).wait_recv()
-            to_z[t][zz] = joined(t, zz).astype(BF16)
-            go(to_z[t].at[zz], from_z[t].at[z], z_send.at[t, zz], z_recv.at[t, z], zdev(zz))
-
-    def finish(t):
-        remote(*x_copy(t, z)).wait_recv()
-        total = joined(t, z)
+            go(to_z[i].at[place(zz)], from_z[i].at[place(z)], z_send.at[i, zz], z_recv.at[i, z], zdev(zz))
+
+    def finish(i):
+        total = parts[i][mine, :].astype(F32)
+        total = total + from_core[i][0, place(z), :].astype(F32) + from_x[i][place(z), :].astype(F32)
         for zz in near:
-            remote(
-                to_z[t].at[zz], from_z[t].at[zz], z_send.at[t, zz], z_recv.at[t, zz], zdev(zz)
-            ).wait_recv()
-            total = total + from_z[t][zz].astype(F32)
+            block = from_z[i].at[place(zz)]
+            remote(to_z[i].at[place(zz)], block, z_send.at[i, zz], z_recv.at[i, zz], zdev(zz)).wait_recv()
+            total = total + block[...].astype(F32)
         return total
 
     own_go(0)
-    for s in range(1, n):
+    pass_z(0, 1)
+    own_go_z(1)
+    for s in range(2, n):
         pass_z(0, s)
-        if s == 1:
-            own_go(1)
-        if s == 2:
-            pass_z(1, 1)
+    own_go_near(1)
+    pass_z(1, 1)
     pass_x(0)
-    for s in range(min(2, n - 1), n):
-        pass_z(1, s)
+    if n > 2:
+        pass_z(1, 2)
     load_gu.wait()
     load_d.wait()
     await_sibling(0, False)
     await_sibling(0, True)
-    forward()
-    core_go(0, True)
-    core_go(0, False)
+    forward_hidden()
+    for s in range(3, n):
+        pass_z(1, s)
+    weight = my_weight()
+    for j in range(tiles):
+        forward_tile(j, weight)
+        core_go(j)
+        if j > 0:
+            x_stage(j - 1)
     pass_x(1)
-    send_x(0)
+    x_stage(tiles - 1)
     await_sibling(1, False)
     await_sibling(1, True)
-    backward()
-    core_go(1, True)
-    core_go(1, False)
-    send_z(0)
-    send_x(1)
-    mixed_ref[...] = finish(0).astype(mixed_ref.dtype)
-    send_z(1)
-    total = finish(1)
-    grad_ref[...] = total[:, :width].astype(grad_ref.dtype)
-    dots = total[:, width:]
-    place = lax.broadcasted_iota(jnp.int32, (tok, top), 1)
+    backward_hidden(weight)
+    core_go(tiles)
+    for j in range(tiles):
+        backward_tile(j)
+        core_go(tiles + 1 + j)
+        x_stage(tiles + j)
+        z_stage(j)
+    x_stage(2 * tiles)
+    for i in range(tiles, 2 * tiles + 1):
+        z_stage(i)
+    for j in range(tiles):
+        mixed_ref[:, j * tile : (j + 1) * tile] = finish(j).astype(mixed_ref.dtype)
+    dots = finish(tiles)
+    for j in range(tiles):
+        grad_ref[:, j * tile : (j + 1) * tile] = finish(tiles + 1 + j).astype(grad_ref.dtype)
+    choice = lax.broadcasted_iota(jnp.int32, (tok, top), 1)
     picked = jnp.zeros((tok, top), F32)
     for k in range(top):
         value = jnp.sum(jnp.where(ids[:, k : k + 1] == lane_expert, dots, 0.0), axis=1, keepdims=True)
-        picked = picked + jnp.where(place == k, value, 0.0)
+        picked = picked + jnp.where(choice == k, value, 0.0)
     gcomb_ref[...] = picked.T
     for copy in sends:
         copy.wait_send()
@@ -446,8 +441,15 @@
     vmem = pl.BlockSpec(memory_space=pltpu.VMEM)
     hbm = pl.BlockSpec(memory_space=pl.ANY)
     dma = pltpu.SemaphoreType.DMA
+    tiles = 4 if width % 1024 == 0 else 1
+    count = 2 * tiles + 1
+
+    def pieces(*lead):
+        sums = [pltpu.VMEM((*lead, width // tiles), BF16)] * tiles
+        return [*sums, pltpu.VMEM((*lead, LANES), BF16), *sums]
+
     mixed, grads, dots = pl.pallas_call(
-        functools.partial(dense_kernel, n),
+        functools.partial(dense_kernel, n, tiles),
         out_shape=(
             jax.ShapeDtypeStruct((tok, width), BF16),
             jax.ShapeDtypeStruct((tok, width), BF16),
@@ -462,32 +464,26 @@
             pltpu.VMEM((ff, width), BF16),
             pltpu.VMEM((total, wide), BF16),
             pltpu.VMEM((total, width), BF16),
-            pltpu.VMEM((total, width), BF16),
-            pltpu.VMEM((total, wide), BF16),
             pltpu.VMEM((total, ff), F32),
             pltpu.VMEM((total, ff), F32),
             pltpu.VMEM((total, ff), BF16),
             pltpu.VMEM((total, 2 * ff), BF16),
-            pltpu.VMEM((2, n * tok, width), BF16),
-            pltpu.VMEM((2, n * tok, wide), BF16),
-            pltpu.VMEM((n, tok, width), BF16),
-            pltpu.VMEM((n, tok, wide), BF16),
-            pltpu.VMEM((n, tok, width), BF16),
-            pltpu.VMEM((n, tok, wide), BF16),
-            pltpu.VMEM((n, tok, width), BF16),
-            pltpu.VMEM((n, tok, wide), BF16),
-            pltpu.VMEM((n, tok, width), BF16),
-            pltpu.VMEM((n, tok, wide), BF16),
+            pieces(total),
+            pieces(2, n * tok),
+            pieces(n * tok),
+            pieces(n * tok),
+            pieces(n * tok),
+            pieces(n * tok),
             dma((6,)),
             dma((2, n)),
             dma((2, 4, n)),
             dma((2, 4, n)),
-            dma((2, 2)),
-            dma((2, 2)),
-            dma((2, n)),
-            dma((2, n)),
-            dma((2, n)),
-            dma((2, n)),
+            dma((count, 2)),
+            dma((count, 2)),
+            dma((count,)),
+            dma((count,)),
+            dma((count, n)),
+            dma((count, n)),
         ],
         compiler_params=pltpu.CompilerParams(
             collective_id=0, has_side_effects=True, vmem_limit_bytes=62 * 1024 * 1024

time: 46.2 us -> 48.1 us (1.041)
  Pallas kernels: 41.1 us -> 43 us
    pallas_call x1, Pallas kernels: 41.1 us -> 43 us  [dense_plan(): pl.pallas_call(functools.partial(dense_kernel, n, tiles), out_shape=(jax....]
where the time goes in v5:
time: 48.1 us; the launch traced here: 47.8 us
  Pallas kernels  43 us (89%)
  local copies, waits for them, and re-layouts  4.22 us (9%)
  between operations  0.64 us (1%)
    pallas_call x1, Pallas kernels, dense_plan(): pl.pallas_call(functools.partial(dense_kernel, n, tiles), out_shape=(jax....  43 us
    unnamed x3, local copies, waits for them, and re-layouts  4.22 us

profile of v5, /device:TPU:0, one launch (start us, length us, event | category | flops | bytes accessed | tf_op | source)
XLA Modules:
  0.0 47.8 jit_solution(5690009322638155920)
XLA Ops:
  0.6 43.0 %shard_map.85 = (bf16[16,2048]{1,0:T(8,128)(2,1)}, bf16[16,2048]{1,0:T(8,128)(2,1)}, f32[8,16]{1,0:T(8,128)}) custom-call(bf16[16,2048]{1,0:T(8,128)(2,1)} %tok_hbm.1, bf16[16,2048]{1,0:T(8,128)(2,1)} %cot_hbm.1, s32[8,16]{1,0:T(8,128)} %bitcast.3, f32[8,16]{1,0:T(8,128)} %bitcast.4, bf16[1,2048,768]{2,1,0:T(8,128)(2,1)} %gate_up_hbm.1, ...), custom_call_target="tpu_custom_call" | custom-call | tf_op jit(solution)/shard_map/pallas_call | solution.py:451
  43.6 1.5 %copy.12 = bf16[16,2048]{1,0:T(8,128)(2,1)} copy(bf16[16,2048]{1,0:T(8,128)(2,1)} %get-tuple-element.12) | data formatting | bytes 131072
  45.1 1.5 %copy.13 = bf16[16,2048]{1,0:T(8,128)(2,1)} copy(bf16[16,2048]{1,0:T(8,128)(2,1)} %get-tuple-element.13) | data formatting | bytes 131072
  46.6 1.3 %copy.14 = f32[16,8]{0,1:T(8,128)} copy(f32[16,8]{0,1:T(8,128)} %bitcast.5) | data formatting | bytes 1024

commit v6 on v4

--- a/solution.py
+++ b/solution.py
@@ -268,6 +268,15 @@
         gather_go(t, 1, z, mine, partner)
         gather_go(t, 2, z, mine, sibling)
 
+    paired = n % 2 == 0 and n >= 4
+    mate = z + 1 - 2 * lax.rem(z, 2)
+    at_end = (z == 0) | (z == n - 1)
+
+    def over_x(t, zz):
+        if not paired:
+            return zz >= 0
+        return (zz != mate) | at_end if t == 0 else zz != mate
+
     def pass_z(t, s):
         for side in (-1, 1):
             here = inside(z + side * s)
@@ -279,13 +288,17 @@
             if s < n - 1:
                 device = zdev(jnp.clip(to, 0, n - 1))
                 go_if(here & inside(to), block, block, ag_send.at[t, 0, zz], ag_recv.at[t, 0, zz], device)
-            go_if(here, block, block, ag_send.at[t, 1, zz], ag_recv.at[t, 1, zz], partner)
+            go_if(here & over_x(t, zz), block, block, ag_send.at[t, 1, zz], ag_recv.at[t, 1, zz], partner)
             go_if(here, block, block, ag_send.at[t, 2, zz], ag_recv.at[t, 2, zz], sibling)
 
     def pass_x(t):
         for zz in [z] + near:
             where = rows(1 - x, c, zz)
             gather_wait(t, 1, zz, where)
+            if paired and zz is z:
+                block = bufs[t].at[where]
+                give = (mate > 0) & (mate < n - 1) if t == 0 else z >= 0
+                go_if(give, block, block, nd_send.at[t, 2], ag_recv.at[t, 1, z], zdev(mate))
             gather_go(t, 3, zz, where, sibling)
 
     def await_sibling(t, other):
@@ -434,6 +447,18 @@
         copy.wait_send()
     for cond, copy in maybe:
         pl.when(cond)(copy.wait_send)
+
+
+def copy_kernel(mixed_ref, grad_ref, dots_ref, mixed_out, grad_out, dots_out, sem):
+    copies = [
+        pltpu.make_async_copy(mixed_ref, mixed_out, sem.at[0]),
+        pltpu.make_async_copy(grad_ref, grad_out, sem.at[1]),
+        pltpu.make_async_copy(dots_ref, dots_out, sem.at[2]),
+    ]
+    for copy in copies:
+        copy.start()
+    for copy in copies:
+        copy.wait()
 
 
 def dense_plan(tokens, cotangent, expert_ids, combine, w_gate_up, w_down):
@@ -479,7 +504,7 @@
             pltpu.VMEM((n, tok, width), BF16),
             pltpu.VMEM((n, tok, wide), BF16),
             dma((6,)),
-            dma((2, n)),
+            dma((2, 3)),
             dma((2, 4, n)),
             dma((2, 4, n)),
             dma((2, 2)),
@@ -493,6 +518,14 @@
             collective_id=0, has_side_effects=True, vmem_limit_bytes=62 * 1024 * 1024
         ),
     )(tokens, cotangent, expert_ids.T, combine.T, w_gate_up, w_down)
+    mixed, grads, dots = pl.pallas_call(
+        copy_kernel,
+        out_shape=tuple(jax.ShapeDtypeStruct(a.shape, a.dtype) for a in (mixed, grads, dots)),
+        in_specs=[hbm] * 3,
+        out_specs=(hbm,) * 3,
+        scratch_shapes=[dma((3,))],
+        compiler_params=pltpu.CompilerParams(vmem_limit_bytes=62 * 1024 * 1024),
+    )(mixed, grads, dots)
     return mixed, grads, dots.T
 
 

time: 46.2 us -> 51.5 us (1.11)
  Pallas kernels: 41.1 us -> 50.6 us
  local copies, waits for them, and re-layouts: 4.22 us -> 0 us
    pallas_call x0 -> x1, Pallas kernels: none -> 5.22 us  [dense_plan(): pl.pallas_call(copy_kernel, out_shape=tuple((jax.ShapeDtypeStruct(a.shape...]
    pallas_call x1, Pallas kernels: 41.1 us -> 45.4 us  [dense_plan(): pl.pallas_call(functools.partial(dense_kernel, n), out_shape=(jax.ShapeDt...]
    unnamed x3 -> x0, local copies, waits for them, and re-layouts: 4.22 us -> none
where the time goes in v6:
time: 51.5 us; the launch traced here: 51.3 us
  Pallas kernels  50.6 us (98%)
  between operations  0.64 us (1%)
    pallas_call x1, Pallas kernels, dense_plan(): pl.pallas_call(functools.partial(dense_kernel, n), out_shape=(jax.ShapeDt...  45.4 us
    pallas_call x1, Pallas kernels, dense_plan(): pl.pallas_call(copy_kernel, out_shape=tuple((jax.ShapeDtypeStruct(a.shape...  5.22 us

profile of v6, /device:TPU:0, one launch (start us, length us, event | category | flops | bytes accessed | tf_op | source)
XLA Modules:
  0.0 51.3 jit_solution(12926861501886402076)
XLA Ops:
  0.6 45.4 %shard_map.85 = (bf16[16,2048]{1,0:T(8,128)(2,1)}, bf16[16,2048]{1,0:T(8,128)(2,1)}, f32[8,16]{1,0:T(8,128)}) custom-call(bf16[16,2048]{1,0:T(8,128)(2,1)} %tok_hbm.1, bf16[16,2048]{1,0:T(8,128)(2,1)} %cot_hbm.1, s32[8,16]{1,0:T(8,128)} %bitcast.3, f32[8,16]{1,0:T(8,128)} %bitcast.4, bf16[1,2048,768]{2,1,0:T(8,128)(2,1)} %gate_up_hbm.1, ...), custom_call_target="tpu_custom_call" | custom-call | tf_op jit(solution)/shard_map/pallas_call | solution.py:474
  46.0 5.2 %shard_map.86 = (bf16[16,2048]{1,0:T(8,128)(2,1)}, bf16[16,2048]{1,0:T(8,128)(2,1)}, f32[8,16]{1,0:T(8,128)}) custom-call(bf16[16,2048]{1,0:T(8,128)(2,1)} %get-tuple-element.9.mixed_ref, bf16[16,2048]{1,0:T(8,128)(2,1)} %get-tuple-element.10.grad_ref, f32[8,16]{1,0:T(8,128)} %get-tuple-element.11.dots_ref), custom_call_target="tpu_custom_call" | custom-call | tf_op jit(solution)/shard_map/pallas_call | solution.py:521

commit v7 on v4

--- a/solution.py
+++ b/solution.py
@@ -282,8 +282,8 @@
             go_if(here, block, block, ag_send.at[t, 1, zz], ag_recv.at[t, 1, zz], partner)
             go_if(here, block, block, ag_send.at[t, 2, zz], ag_recv.at[t, 2, zz], sibling)
 
-    def pass_x(t):
-        for zz in [z] + near:
+    def pass_x(t, places):
+        for zz in places:
             where = rows(1 - x, c, zz)
             gather_wait(t, 1, zz, where)
             gather_go(t, 3, zz, where, sibling)
@@ -302,7 +302,7 @@
         chosen = (wide_lane == me) | (wide_lane == me + experts)
         return jnp.sum(jnp.where(chosen, block, 0.0), axis=1, keepdims=True)
 
-    def forward():
+    def forward_hidden():
         projected = jnp.dot(xs[:, :width], wgu[...], preferred_element_type=F32)
         gate = projected[:, :ff]
         upward = projected[:, ff:]
@@ -310,6 +310,8 @@
         gate_s[...] = gate
         up_s[...] = upward
         hid_s[...] = hidden
+
+    def forward_out():
         weight = my_weight()
 
         @pl.loop(0, width // tile)
@@ -320,7 +322,7 @@
 
     across = (((1,), (1,)), ((), ()))
 
-    def backward():
+    def backward_hidden():
         plain = lax.dot_general(cs[...], wd[...], across, preferred_element_type=F32)
         gate = gate_s[...]
         upward = up_s[...]
@@ -336,6 +338,7 @@
         pair_s[:, :ff] = grad_gate.astype(BF16)
         pair_s[:, ff:] = grad_up.astype(BF16)
 
+    def backward_out():
         @pl.loop(0, width // tile)
         def _(j):
             cols = pl.ds(pl.multiple_of(j * tile, tile), tile)
@@ -366,11 +369,17 @@
     order = far + [z]
 
     def send_x(t):
+        started = []
         core_wait(t, True)
-        for zz in order:
+        for i, zz in enumerate(order):
             own = parts[t][rows(1 - x, c, zz), :].astype(F32)
             to_x[t][zz] = (own + from_core[t][1, core_rows(zz), :].astype(F32)).astype(BF16)
-            go(*x_copy(t, zz))
+            copy = remote(*x_copy(t, zz))
+            copy.start()
+            started.append(copy)
+            if t == 1 and i >= 1:
+                started[i - 1].wait_send()
+        sends.extend(started if t == 0 else started[-1:])
 
     def joined(t, zz):
         own = parts[t][rows(x, c, zz), :].astype(F32)
@@ -400,24 +409,27 @@
             own_go(1)
         if s == 2:
             pass_z(1, 1)
-    pass_x(0)
-    for s in range(min(2, n - 1), n):
-        pass_z(1, s)
+    pass_x(0, [z] + near)
     load_gu.wait()
     load_d.wait()
     await_sibling(0, False)
     await_sibling(0, True)
-    forward()
+    forward_hidden()
+    for s in range(min(2, n - 1), n):
+        pass_z(1, s)
+    forward_out()
     core_go(0, True)
     core_go(0, False)
-    pass_x(1)
+    pass_x(1, [z] + near[:1])
     send_x(0)
+    pass_x(1, near[1:])
     await_sibling(1, False)
     await_sibling(1, True)
-    backward()
+    backward_hidden()
+    send_z(0)
+    backward_out()
     core_go(1, True)
     core_go(1, False)
-    send_z(0)
     send_x(1)
     mixed_ref[...] = finish(0).astype(mixed_ref.dtype)
     send_z(1)

time: 46.2 us -> 49.7 us (1.076)
  Pallas kernels: 41.1 us -> 44.6 us
    pallas_call x1, Pallas kernels: 41.1 us -> 44.6 us  [dense_plan(): pl.pallas_call(functools.partial(dense_kernel, n), out_shape=(jax.ShapeDt...]
where the time goes in v7:
time: 49.7 us; the launch traced here: 49.4 us
  Pallas kernels  44.6 us (90%)
  local copies, waits for them, and re-layouts  4.22 us (8%)
  between operations  0.64 us (1%)
    pallas_call x1, Pallas kernels, dense_plan(): pl.pallas_call(functools.partial(dense_kernel, n), out_shape=(jax.ShapeDt...  44.6 us
    unnamed x3, local copies, waits for them, and re-layouts  4.22 us

profile of v7, /device:TPU:0, one launch (start us, length us, event | category | flops | bytes accessed | tf_op | source)
XLA Modules:
  0.0 49.4 jit_solution(12474297132825834897)
XLA Ops:
  0.6 44.6 %shard_map.85 = (bf16[16,2048]{1,0:T(8,128)(2,1)}, bf16[16,2048]{1,0:T(8,128)(2,1)}, f32[8,16]{1,0:T(8,128)}) custom-call(bf16[16,2048]{1,0:T(8,128)(2,1)} %tok_hbm.1, bf16[16,2048]{1,0:T(8,128)(2,1)} %cot_hbm.1, s32[8,16]{1,0:T(8,128)} %bitcast.3, f32[8,16]{1,0:T(8,128)} %bitcast.4, bf16[1,2048,768]{2,1,0:T(8,128)(2,1)} %gate_up_hbm.1, ...), custom_call_target="tpu_custom_call" | custom-call | tf_op jit(solution)/shard_map/pallas_call | solution.py:461
  45.2 1.5 %copy.12 = bf16[16,2048]{1,0:T(8,128)(2,1)} copy(bf16[16,2048]{1,0:T(8,128)(2,1)} %get-tuple-element.12) | data formatting | bytes 131072
  46.7 1.5 %copy.13 = bf16[16,2048]{1,0:T(8,128)(2,1)} copy(bf16[16,2048]{1,0:T(8,128)(2,1)} %get-tuple-element.13) | data formatting | bytes 131072
  48.1 1.3 %copy.14 = f32[16,8]{0,1:T(8,128)} copy(f32[16,8]{0,1:T(8,128)} %bitcast.5) | data formatting | bytes 1024

commit v8 on v7

--- a/solution.py
+++ b/solution.py
@@ -369,17 +369,11 @@
     order = far + [z]
 
     def send_x(t):
-        started = []
         core_wait(t, True)
-        for i, zz in enumerate(order):
+        for zz in order:
             own = parts[t][rows(1 - x, c, zz), :].astype(F32)
             to_x[t][zz] = (own + from_core[t][1, core_rows(zz), :].astype(F32)).astype(BF16)
-            copy = remote(*x_copy(t, zz))
-            copy.start()
-            started.append(copy)
-            if t == 1 and i >= 1:
-                started[i - 1].wait_send()
-        sends.extend(started if t == 0 else started[-1:])
+            go(*x_copy(t, zz))
 
     def joined(t, zz):
         own = parts[t][rows(x, c, zz), :].astype(F32)
@@ -410,26 +404,25 @@
         if s == 2:
             pass_z(1, 1)
     pass_x(0, [z] + near)
+    for s in range(min(2, n - 1), n):
+        pass_z(1, s)
     load_gu.wait()
     load_d.wait()
     await_sibling(0, False)
     await_sibling(0, True)
     forward_hidden()
-    for s in range(min(2, n - 1), n):
-        pass_z(1, s)
+    pass_x(1, [z] + near)
     forward_out()
     core_go(0, True)
     core_go(0, False)
-    pass_x(1, [z] + near[:1])
-    send_x(0)
-    pass_x(1, near[1:])
     await_sibling(1, False)
     await_sibling(1, True)
     backward_hidden()
-    send_z(0)
+    send_x(0)
     backward_out()
     core_go(1, True)
     core_go(1, False)
+    send_z(0)
     send_x(1)
     mixed_ref[...] = finish(0).astype(mixed_ref.dtype)
     send_z(1)

time: 49.7 us -> 50.2 us (1.010)
    pallas_call x1, Pallas kernels: 44.6 us -> 45.1 us  [dense_plan(): pl.pallas_call(functools.partial(dense_kernel, n), out_shape=(jax.ShapeDt...]
where the time goes in v8:
time: 50.2 us; the launch traced here: 49.9 us
  Pallas kernels  45.1 us (90%)
  local copies, waits for them, and re-layouts  4.22 us (8%)
  between operations  0.64 us (1%)
    pallas_call x1, Pallas kernels, dense_plan(): pl.pallas_call(functools.partial(dense_kernel, n), out_shape=(jax.ShapeDt...  45.1 us
    unnamed x3, local copies, waits for them, and re-layouts  4.22 us

profile of v8, /device:TPU:0, one launch (start us, length us, event | category | flops | bytes accessed | tf_op | source)
XLA Modules:
  0.0 49.9 jit_solution(18126618662016602468)
XLA Ops:
  0.6 45.1 %shard_map.85 = (bf16[16,2048]{1,0:T(8,128)(2,1)}, bf16[16,2048]{1,0:T(8,128)(2,1)}, f32[8,16]{1,0:T(8,128)}) custom-call(bf16[16,2048]{1,0:T(8,128)(2,1)} %tok_hbm.1, bf16[16,2048]{1,0:T(8,128)(2,1)} %cot_hbm.1, s32[8,16]{1,0:T(8,128)} %bitcast.3, f32[8,16]{1,0:T(8,128)} %bitcast.4, bf16[1,2048,768]{2,1,0:T(8,128)(2,1)} %gate_up_hbm.1, ...), custom_call_target="tpu_custom_call" | custom-call | tf_op jit(solution)/shard_map/pallas_call | solution.py:454
  45.7 1.5 %copy.12 = bf16[16,2048]{1,0:T(8,128)(2,1)} copy(bf16[16,2048]{1,0:T(8,128)(2,1)} %get-tuple-element.12) | data formatting | bytes 131072
  47.2 1.5 %copy.13 = bf16[16,2048]{1,0:T(8,128)(2,1)} copy(bf16[16,2048]{1,0:T(8,128)(2,1)} %get-tuple-element.13) | data formatting | bytes 131072
  48.7 1.3 %copy.14 = f32[16,8]{0,1:T(8,128)} copy(f32[16,8]{0,1:T(8,128)} %bitcast.5) | data formatting | bytes 1024

commit v9 on v4

--- a/solution.py
+++ b/solution.py
@@ -282,8 +282,8 @@
             go_if(here, block, block, ag_send.at[t, 1, zz], ag_recv.at[t, 1, zz], partner)
             go_if(here, block, block, ag_send.at[t, 2, zz], ag_recv.at[t, 2, zz], sibling)
 
-    def pass_x(t):
-        for zz in [z] + near:
+    def pass_x(t, places):
+        for zz in places:
             where = rows(1 - x, c, zz)
             gather_wait(t, 1, zz, where)
             gather_go(t, 3, zz, where, sibling)
@@ -400,7 +400,7 @@
             own_go(1)
         if s == 2:
             pass_z(1, 1)
-    pass_x(0)
+    pass_x(0, [z] + near)
     for s in range(min(2, n - 1), n):
         pass_z(1, s)
     load_gu.wait()
@@ -410,8 +410,9 @@
     forward()
     core_go(0, True)
     core_go(0, False)
-    pass_x(1)
+    pass_x(1, [z] + near[:1])
     send_x(0)
+    pass_x(1, near[1:])
     await_sibling(1, False)
     await_sibling(1, True)
     backward()

time: 46.2 us -> 47.7 us (1.032)
  Pallas kernels: 41.1 us -> 42.6 us
    pallas_call x1, Pallas kernels: 41.1 us -> 42.6 us  [dense_plan(): pl.pallas_call(functools.partial(dense_kernel, n), out_shape=(jax.ShapeDt...]
where the time goes in v9:
time: 47.7 us; the launch traced here: 47.5 us
  Pallas kernels  42.6 us (89%)
  local copies, waits for them, and re-layouts  4.22 us (9%)
  between operations  0.64 us (1%)
    pallas_call x1, Pallas kernels, dense_plan(): pl.pallas_call(functools.partial(dense_kernel, n), out_shape=(jax.ShapeDt...  42.6 us
    unnamed x3, local copies, waits for them, and re-layouts  4.22 us

profile of v9, /device:TPU:0, one launch (start us, length us, event | category | flops | bytes accessed | tf_op | source)
XLA Modules:
  0.0 47.5 jit_solution(16293908803334537879)
XLA Ops:
  0.6 42.6 %shard_map.85 = (bf16[16,2048]{1,0:T(8,128)(2,1)}, bf16[16,2048]{1,0:T(8,128)(2,1)}, f32[8,16]{1,0:T(8,128)}) custom-call(bf16[16,2048]{1,0:T(8,128)(2,1)} %tok_hbm.1, bf16[16,2048]{1,0:T(8,128)(2,1)} %cot_hbm.1, s32[8,16]{1,0:T(8,128)} %bitcast.3, f32[8,16]{1,0:T(8,128)} %bitcast.4, bf16[1,2048,768]{2,1,0:T(8,128)(2,1)} %gate_up_hbm.1, ...), custom_call_target="tpu_custom_call" | custom-call | tf_op jit(solution)/shard_map/pallas_call | solution.py:450
  43.2 1.5 %copy.12 = bf16[16,2048]{1,0:T(8,128)(2,1)} copy(bf16[16,2048]{1,0:T(8,128)(2,1)} %get-tuple-element.12) | data formatting | bytes 131072
  44.7 1.5 %copy.13 = bf16[16,2048]{1,0:T(8,128)(2,1)} copy(bf16[16,2048]{1,0:T(8,128)(2,1)} %get-tuple-element.13) | data formatting | bytes 131072
  46.2 1.3 %copy.14 = f32[16,8]{0,1:T(8,128)} copy(f32[16,8]{0,1:T(8,128)} %bitcast.5) | data formatting | bytes 1024
